TPU v7x, 32 devices: a whole 2x2x4 slice. The times are simulated.
32 devices in a mesh: dp: 8 (over z, y), mp: 4 (over x, core).
Axes of the slice: x: 2, y: 2, z: 4, core: 2. Of those that a mesh axis runs over, the one named last changes fastest.
Arguments:
- tokens: bfloat16 [4096, 1152], P(('dp', 'mp')), may hold values from -6 to 6
- segment_ids: int32 [4096], P('dp'), may hold values from 0 to 2, as said below
- positions: int32 [4096], P('dp'), may hold values from 0 to 5118, as said below
- q_weight: bfloat16 [1152, 1024], P('dp', 'mp'), may hold values from -0.1875 to 0.1875
- kv_weight: bfloat16 [1152, 512], P('dp'), may hold values from -0.1875 to 0.1875
- o_weight: bfloat16 [1024, 1152], P('mp', 'dp'), may hold values from -0.1875 to 0.1875
- gate_up_weight: bfloat16 [2, 1152, 6912], P(None, 'dp', 'mp'), may hold values from -0.1875 to 0.1875
- down_weight: bfloat16 [6912, 1152], P('mp', 'dp'), may hold values from -0.078125 to 0.078125
- attn_pre_gain: bfloat16 [1152], P('dp'), may hold values from 0.25 to 1.75
- attn_post_gain: bfloat16 [1152], P('dp'), may hold values from 0.25 to 1.75
- ff_pre_gain: bfloat16 [1152], P('dp'), may hold values from 0.25 to 1.75
- ff_post_gain: bfloat16 [1152], P('dp'), may hold values from 0.25 to 1.75
- query_gain: bfloat16 [256], P('dp'), may hold values from 0.25 to 1.75
- key_gain: bfloat16 [256], P('dp'), may hold values from 0.25 to 1.75
- out_grad: bfloat16 [4096, 1152], P(('dp', 'mp')), may hold values from -6 to 6
Outputs:
- out: bfloat16 [4096, 1152], P(('dp', 'mp'))
- tokens_grad: float32 [4096, 1152], P(('dp', 'mp'))
- q_weight_grad: float32 [1152, 1024], P('dp', 'mp')
- kv_weight_grad: float32 [1152, 512], P('dp')
- o_weight_grad: float32 [1024, 1152], P('mp', 'dp')
- gate_up_weight_grad: float32 [2, 1152, 6912], P(None, 'dp', 'mp')
- down_weight_grad: float32 [6912, 1152], P('mp', 'dp')
- attn_pre_gain_grad: float32 [1152], P('dp')
- attn_post_gain_grad: float32 [1152], P('dp')
- ff_pre_gain_grad: float32 [1152], P('dp')
- ff_post_gain_grad: float32 [1152], P('dp')
- query_gain_grad: float32 [256], P('dp')
- key_gain_grad: float32 [256], P('dp')
Inputs may be any that keep to these rules, and one draw needn't show every extreme that they name: `segment_ids`: segment ids never fall; document 0 and document 2 each hold 1 to 256 tokens, document 1 the rest. Within a document, positions rise by one from token to token; document 0 starts at position 0, document 2 at 0 to 1023, and the last token of document 1 has position 5118.
All inputs are finite; a program needn't handle non-finite values.
Results may differ from a plain program's by a relative error of at most 0.028.
Values may be sent and summed in bfloat16 or wider, within the bound.
A program may use at most 128 MiB of HBM per device.

v0:
```python
from functools import partial
import jax
import jax.numpy as jnp
from jax import lax
from jax.sharding import PartitionSpec as P

WINDOW = 512
EPS = 1e-06
NEG = -1e30


def from_behind(value, axis, steps):
    count = lax.axis_size(axis)
    leading, last = (max(0, -steps), min(count, count - steps))
    return lax.ppermute(value, axis, [(source, source + steps) for source in range(leading, last)])


def shifted(value, axis, shift):
    count = lax.axis_size(axis)
    return lax.ppermute(value, axis, [(i, (i + shift) % count) for i in range(count)])


def gather_relative(value):
    count = lax.axis_size("mp")
    return [value] + [shifted(value, "mp", -step) for step in range(1, count)]


def gather_ordered(value):
    count = lax.axis_size("mp")
    rows = value.shape[0]
    me = lax.axis_index("mp")
    whole = jnp.zeros((count * rows,) + value.shape[1:], value.dtype)
    for step, block in enumerate(gather_relative(value)):
        owner = lax.rem(me + step, count)
        whole = lax.dynamic_update_slice_in_dim(whole, block, owner * rows, axis=0)
    return whole


def scatter_relative(blocks):
    total = blocks[0].astype(jnp.float32)
    for step in range(1, len(blocks)):
        total = total + shifted(blocks[step], "mp", step).astype(jnp.float32)
    return total


def scatter_ordered(value):
    count = lax.axis_size("mp")
    rows = value.shape[0] // count
    me = lax.axis_index("mp")
    return scatter_relative(
        [
            lax.dynamic_slice_in_dim(value, lax.rem(me + step, count) * rows, rows, axis=0)
            for step in range(count)
        ]
    )


def split_rows(value):
    rows = value.shape[0] // lax.axis_size("mp")
    return [value[i * rows : (i + 1) * rows] for i in range(lax.axis_size("mp"))]


def sum_over_mp(value):
    total = value.astype(jnp.float32)
    for step in range(1, lax.axis_size("mp")):
        total = total + shifted(value, "mp", step).astype(jnp.float32)
    return total


def normalize(value, gain):
    return value * lax.rsqrt(jnp.mean(value * value, axis=-1, keepdims=True) + EPS) * gain


def rotary_tables(positions, width):
    half_width = width // 2
    frequency = jnp.power(10000.0, -jnp.arange(half_width, dtype=jnp.float32) * (2.0 / width))
    angles = positions.astype(jnp.float32)[:, None] * frequency[None, :]
    return (jnp.cos(angles), jnp.sin(angles))


def rotate(value, cosine, sine):
    half_width = value.shape[-1] // 2
    first_half = value[..., :half_width]
    second_half = value[..., half_width:]
    return jnp.concatenate(
        [first_half * cosine - second_half * sine, second_half * cosine + first_half * sine],
        axis=-1,
    )


def prepare_head(pre_value, gain, cosine, sine):
    return rotate(normalize(pre_value, gain), cosine, sine)


def gated_units(gate, up_part):
    return jax.nn.gelu(gate, approximate=True) * up_part


def norm_back(value, gain, grad):
    unused, pull = jax.vjp(normalize, value, gain)
    return pull(grad)


def local(
    tokens,
    segment_ids,
    positions,
    q_weight,
    kv_weight,
    o_weight,
    gate_up_weight,
    down_weight,
    attn_pre_gain,
    attn_post_gain,
    ff_pre_gain,
    ff_post_gain,
    query_gain,
    key_gain,
    out_grad,
):
    rows = q_weight.shape[0]
    head_size = q_weight.shape[1]
    width = rows * lax.axis_size("dp")
    gain_rows = query_gain.shape[0]
    small_gains = [jnp.pad(item, (0, rows - gain_rows)) for item in (query_gain, key_gain)]
    gain_columns = jnp.stack(
        [attn_pre_gain, attn_post_gain, ff_pre_gain, ff_post_gain] + small_gains, axis=1
    )
    gain_columns = jnp.pad(gain_columns, ((0, 0), (0, 128 - gain_columns.shape[1])))
    packed = jnp.concatenate([q_weight, kv_weight, jnp.transpose(o_weight), gain_columns], axis=1)
    packed_full = lax.all_gather(packed, "dp", axis=0, tiled=True)
    gate_up_full = lax.all_gather(gate_up_weight, "dp", axis=1, tiled=True)
    down_full = lax.all_gather(down_weight, "dp", axis=1, tiled=True)
    joint_weight = packed_full[:, : 3 * head_size]
    output_turned = packed_full[:, 3 * head_size : 4 * head_size]
    gain_block = jnp.transpose(packed_full[:, 4 * head_size :]).astype(jnp.float32)
    gains = [gain_block[i] for i in range(4)] + [
        gain_block[i].reshape(-1, rows)[:, :gain_rows].reshape(-1) for i in (4, 5)
    ]
    length = segment_ids.shape[0]
    reach = -(-WINDOW // length)
    block_size = min(512, length)
    score_scale = head_size ** (-0.5)
    span = block_size + WINDOW
    cosine, sine = rotary_tables(positions, head_size)
    distance = (
        jnp.arange(block_size, dtype=jnp.int32)[:, None]
        + WINDOW
        - jnp.arange(span, dtype=jnp.int32)[None, :]
    )
    inside = (distance >= 0) & (distance < WINDOW)
    residual = tokens.astype(jnp.float32)
    attn_local = normalize(residual, gains[0]).astype(jnp.bfloat16)
    attn_in = gather_ordered(attn_local)
    projected = jnp.dot(attn_in, joint_weight, preferred_element_type=jnp.float32)
    query_pre = projected[:, :head_size]
    key_pre = projected[:, head_size : 2 * head_size]
    value_pre = projected[:, 2 * head_size :]
    queries = prepare_head(query_pre, gains[4], cosine, sine).astype(jnp.bfloat16)
    keys = prepare_head(key_pre, gains[5], cosine, sine).astype(jnp.bfloat16)
    values = value_pre.astype(jnp.bfloat16)
    marks = (segment_ids + 1).astype(jnp.bfloat16)
    key_parts, value_parts, mark_parts = ([], [], [])
    step = 1
    moved = from_behind((keys, values, marks), "dp", step)
    key_parts.append(moved[0])
    value_parts.append(moved[1])
    mark_parts.append(moved[2])
    all_keys = jnp.concatenate(key_parts + [keys], axis=0)
    all_values = jnp.concatenate(value_parts + [values], axis=0)
    all_marks = jnp.concatenate(mark_parts + [marks], axis=0)

    def block_parts(start):
        first_key = start + reach * length - WINDOW
        visible = inside & (marks[:, None] == all_marks[None, :])
        product = (
            jnp.einsum("qd,kd->qk", queries, all_keys, preferred_element_type=jnp.float32)
            * score_scale
        )
        return (first_key, queries, all_keys, all_values, jnp.where(visible, product, NEG))

    mixed_parts, total_parts = ([], [])
    start = 0
    first_key, query_block, key_block, value_block, scores = block_parts(start)
    highest = jnp.max(scores, axis=-1, keepdims=True)
    expo = jnp.exp(scores - highest)
    denominator = jnp.sum(expo, axis=-1, keepdims=True)
    probs = (expo / denominator).astype(jnp.bfloat16)
    mixed_parts.append(jnp.dot(probs, value_block, preferred_element_type=jnp.float32))
    total_parts.append(highest + jnp.log(denominator))
    attended = mixed_parts[0].astype(jnp.bfloat16)
    log_totals = total_parts[0]
    attn_out = scatter_ordered(
        jnp.einsum("le,de->ld", attended, output_turned, preferred_element_type=jnp.float32).astype(
            jnp.bfloat16
        )
    )
    middle = residual + normalize(attn_out, gains[1])
    ff_local = normalize(middle, gains[2]).astype(jnp.bfloat16)
    ff_in = jnp.concatenate(gather_relative(ff_local), axis=0)
    gate = jnp.dot(ff_in, gate_up_full[0], preferred_element_type=jnp.float32)
    up_part = jnp.dot(ff_in, gate_up_full[1], preferred_element_type=jnp.float32)
    hidden = gated_units(gate, up_part).astype(jnp.bfloat16)
    ff_out = scatter_relative(
        split_rows(
            jnp.dot(hidden, down_full, preferred_element_type=jnp.float32).astype(jnp.bfloat16)
        )
    )
    result = (middle + normalize(ff_out, gains[3])).astype(jnp.bfloat16)
    top_grad = out_grad.astype(jnp.float32)
    ff_out_grad, ff_post_grad = norm_back(ff_out, gains[3], top_grad)
    ff_grad_all = jnp.concatenate(gather_relative(ff_out_grad.astype(jnp.bfloat16)), axis=0)
    hidden_grad = jnp.einsum(
        "ld,fd->lf", ff_grad_all, down_full, preferred_element_type=jnp.float32
    )
    down_grad_turned = jnp.einsum(
        "ld,lf->df", ff_grad_all, hidden, preferred_element_type=jnp.float32
    )
    unused, unit_pull = jax.vjp(gated_units, gate, up_part)
    gate_grad, up_grad = unit_pull(hidden_grad)
    gate_low = gate_grad.astype(jnp.bfloat16)
    up_low = up_grad.astype(jnp.bfloat16)
    gate_turned = jnp.einsum("ld,lf->df", ff_in, gate_low, preferred_element_type=jnp.float32)
    up_turned = jnp.einsum("ld,lf->df", ff_in, up_low, preferred_element_type=jnp.float32)
    ff_in_partial = (
        jnp.einsum("lf,df->ld", gate_low, gate_up_full[0], preferred_element_type=jnp.float32)
        + jnp.einsum("lf,df->ld", up_low, gate_up_full[1], preferred_element_type=jnp.float32)
    ).astype(jnp.bfloat16)
    ff_in_partial, down_low, gate_turned_low, up_turned_low = lax.optimization_barrier(
        (
            ff_in_partial,
            down_grad_turned.astype(jnp.bfloat16),
            gate_turned.astype(jnp.bfloat16),
            up_turned.astype(jnp.bfloat16),
        )
    )
    feed_forward_owned = tuple(
        (
            lax.psum_scatter(item, "dp", scatter_dimension=0, tiled=True)
            for item in (down_low, gate_turned_low, up_turned_low)
        )
    )
    ff_in_grad = scatter_relative(split_rows(ff_in_partial))
    middle_part, ff_pre_grad = norm_back(middle, gains[2], ff_in_grad)
    middle_grad = top_grad + middle_part
    attn_out_grad, attn_post_grad = norm_back(attn_out, gains[1], middle_grad)
    attn_grad_all = gather_ordered(attn_out_grad.astype(jnp.bfloat16))
    attended_grad = jnp.einsum(
        "ld,de->le", attn_grad_all, output_turned, preferred_element_type=jnp.float32
    ).astype(jnp.bfloat16)
    output_grad_turned = jnp.einsum(
        "ld,le->de", attn_grad_all, attended, preferred_element_type=jnp.float32
    )
    key_grad_all = jnp.zeros(((reach + 1) * length, head_size), jnp.float32)
    value_grad_all = jnp.zeros(((reach + 1) * length, head_size), jnp.float32)
    start = 0
    first_key, query_block, key_block, value_block, scores = block_parts(start)
    probs = jnp.exp(scores - log_totals)
    probs_low = probs.astype(jnp.bfloat16)
    value_grad_all = value_grad_all.at[first_key : first_key + span].add(
        jnp.einsum("qk,qd->kd", probs_low, attended_grad, preferred_element_type=jnp.float32)
    )
    prob_grad = jnp.einsum(
        "qd,kd->qk", attended_grad, value_block, preferred_element_type=jnp.float32
    )
    inner = jnp.sum(probs * prob_grad, axis=-1, keepdims=True)
    score_grad = (probs * (prob_grad - inner)).astype(jnp.bfloat16)
    query_parts = jnp.dot(score_grad, key_block, preferred_element_type=jnp.float32) * score_scale
    key_grad_all = key_grad_all.at[first_key : first_key + span].add(
        jnp.einsum("qk,qd->kd", score_grad, query_block, preferred_element_type=jnp.float32)
        * score_scale
    )
    own_keys = key_grad_all[reach * length :]
    own_values = value_grad_all[reach * length :]
    step = 1
    slot = reach - step
    returned = (
        from_behind(
            key_grad_all[slot * length : (slot + 1) * length].astype(jnp.bfloat16), "dp", -step
        ).astype(jnp.float32),
        from_behind(
            value_grad_all[slot * length : (slot + 1) * length].astype(jnp.bfloat16), "dp", -step
        ).astype(jnp.float32),
    )
    own_keys = own_keys + returned[0]
    own_values = own_values + returned[1]
    unused, query_pull = jax.vjp(
        partial(prepare_head, cosine=cosine, sine=sine), query_pre, gains[4]
    )
    query_pre_grad, query_gain_grad = query_pull(query_parts)
    unused, key_pull = jax.vjp(partial(prepare_head, cosine=cosine, sine=sine), key_pre, gains[5])
    key_pre_grad, key_gain_grad = key_pull(own_keys)
    joint_grad_rows = jnp.concatenate([query_pre_grad, key_pre_grad, own_values], axis=1).astype(
        jnp.bfloat16
    )
    joint_grad = jnp.einsum(
        "ld,lc->dc", attn_in, joint_grad_rows, preferred_element_type=jnp.float32
    )
    attn_in_grad = scatter_ordered(
        jnp.einsum(
            "lc,dc->ld", joint_grad_rows, joint_weight, preferred_element_type=jnp.float32
        ).astype(jnp.bfloat16)
    )
    tokens_part, attn_pre_grad = norm_back(residual, gains[0], attn_in_grad)
    tokens_grad = middle_grad + tokens_part
    small_grads = [
        jnp.pad(item.reshape(-1, gain_rows), ((0, 0), (0, rows - gain_rows))).reshape(-1)
        for item in (query_gain_grad, key_gain_grad)
    ]
    gain_grads = jnp.stack(
        [attn_pre_grad, attn_post_grad, ff_pre_grad, ff_post_grad] + small_grads, axis=1
    )
    gain_grads = jnp.pad(gain_grads, ((0, 0), (0, 128 - gain_grads.shape[1])))
    packed_grad = jnp.concatenate(
        [
            joint_grad[:, :head_size].astype(jnp.bfloat16),
            output_grad_turned.astype(jnp.bfloat16),
            joint_grad[:, head_size:].astype(jnp.bfloat16),
            gain_grads.astype(jnp.bfloat16),
        ],
        axis=1,
    )
    packed_grad, feed_forward_owned = lax.optimization_barrier((packed_grad, feed_forward_owned))
    down_owned = jnp.transpose(feed_forward_owned[0]).astype(jnp.float32)
    gate_up_owned = jnp.stack(feed_forward_owned[1:], axis=0).astype(jnp.float32)
    packed_owned = lax.psum_scatter(packed_grad, "dp", scatter_dimension=0, tiled=True)
    query_owned = packed_owned[:, :head_size].astype(jnp.float32)
    output_owned = jnp.transpose(packed_owned[:, head_size : 2 * head_size]).astype(jnp.float32)
    summed = sum_over_mp(packed_owned[:, 2 * head_size :])
    keyval_owned = summed[:, : 2 * head_size]
    gain_owned = jnp.transpose(summed[:, 2 * head_size :])
    return (
        result,
        tokens_grad,
        query_owned,
        keyval_owned,
        output_owned,
        gate_up_owned,
        down_owned,
        gain_owned[0],
        gain_owned[1],
        gain_owned[2],
        gain_owned[3],
        gain_owned[4, :gain_rows],
        gain_owned[5, :gain_rows],
    )


def solution(mesh):
    placed = (
        P(("dp", "mp"), None),
        P("dp"),
        P("dp"),
        P("dp", "mp"),
        P("dp", None),
        P("mp", "dp"),
        P(None, "dp", "mp"),
        P("mp", "dp"),
        P("dp"),
        P("dp"),
        P("dp"),
        P("dp"),
        P("dp"),
        P("dp"),
        P(("dp", "mp"), None),
    )
    return jax.shard_map(
        local,
        mesh=mesh,
        in_specs=placed,
        out_specs=(
            P(("dp", "mp"), None),
            P(("dp", "mp"), None),
            P("dp", "mp"),
            P("dp", None),
            P("mp", "dp"),
            P(None, "dp", "mp"),
            P("mp", "dp"),
            P("dp"),
            P("dp"),
            P("dp"),
            P("dp"),
            P("dp"),
            P("dp"),
        ),
        check_vma=False,
    )
```

profile of v0, /device:TPU:0, one launch (start us, length us, event | category | flops | bytes accessed | tf_op | source)
XLA Modules:
  0.0 732.3 jit_solution(13621012869615528322)
XLA Ops:
  11.4 1.8 fusion.63
  14.2 56.9 %all-gather.4.cloned.1.call-done = bf16[1152,1152]{1,0:T(8,128)(2,1)} async-done(((bf16[144,1152]{1,0:T(8,128)(2,1)}), bf16[1152,1152]{1,0:T(8,128)(2,1)}) %all-gather.4.cloned.1.call-update) | async-done | bytes 2654224 | tf_op jit(solution)/shard_map/all_gather | solution.py:131
  72.1 1.8 slice_reduce_fusion
  74.5 1.5 collective-permute-start.2
  76.5 3.9 collective-permute-done.1
  80.4 9.1 %collective-permute-done.2 = bf16[128,1152]{1,0:T(8,128)(2,1)S(1)} collective-permute-done((bf16[128,1152]{1,0:T(8,128)(2,1)S(1)}, bf16[128,1152]{1,0:T(8,128)(2,1)S(1)}, u32[]{:S(2)}, u32[]{:S(2)}) %collective-permute-start.2) | collective-permute-done | bytes 294944 | tf_op jit(solution)/shard_map/ppermute | solution.py:20
  89.9 3.1 fusion.22
  94.9 2.5 collective-permute-start.4
  97.4 4.3 collective-permute-start
  103.1 10.1 %collective-permute-start.5 = (bf16[512,256]{1,0:T(8,128)(2,1)S(1)}, bf16[512,256]{1,0:T(8,128)(2,1)S(1)}, u32[]{:S(2)}, u32[]{:S(2)}) collective-permute-start(bf16[512,256]{1,0:T(8,128)(2,1)S(1)} %slice.321), channel_id=1, source_target_pairs={{0,4},{4,8},{8,12},{12,16},{16,20},{20,24},{24,28},{1,5},{5,9},{9,... | collective-permute-start | bytes 786440 | tf_op jit(solution)/shard_map/ppermute | solution.py:15
  114.7 2.3 collective-permute-done.5
  117.7 1.7 convolution_convert_fusion.6
  120.8 5.7 collective-permute-done.8
  126.5 7.6 %collective-permute-done.7 = bf16[128,1152]{1,0:T(8,128)(2,1)S(1)} collective-permute-done((bf16[128,1152]{1,0:T(8,128)(2,1)S(1)}, bf16[128,1152]{1,0:T(8,128)(2,1)S(1)}, u32[]{:S(2)}, u32[]{:S(2)}) %collective-permute-start.7) | collective-permute-done | bytes 294944 | tf_op jit(solution)/shard_map/ppermute | solution.py:20
  136.7 1.5 collective-permute-start.9
  138.2 6.0 collective-permute-done.11
  146.2 3.5 collective-permute-done.9
  149.7 54.7 %all-gather.6.cloned.1.call-done = bf16[2,1152,1728]{2,1,0:T(8,128)(2,1)} async-done(((bf16[2,144,1728]{2,1,0:T(8,128)(2,1)}), bf16[2,1152,1728]{2,1,0:T(8,128)(2,1)}) %all-gather.6.cloned.1.call-update) | async-done | bytes 7962640 | tf_op jit(solution)/shard_map/all_gather | solution.py:132
  204.4 5.2 fusion.2
  209.7 1.8 copy-done.76
  211.4 6.8 multiply_convert_fusion.1
  218.2 59.2 %all-gather.8.cloned.1.call-done = bf16[1728,1152]{0,1:T(8,128)(2,1)} async-done(((bf16[1728,144]{0,1:T(8,128)(2,1)}), bf16[1728,1152]{0,1:T(8,128)(2,1)}) %all-gather.8.cloned.1.call-update) | async-done | bytes 3981328 | tf_op jit(solution)/shard_map/all_gather | solution.py:133
  277.4 5.3 convolution_convert_fusion.5
  282.9 1.5 collective-permute-start.13
  284.6 4.7 collective-permute-done.14
  289.2 9.2 %collective-permute-done.13 = bf16[128,1152]{1,0:T(8,128)(2,1)S(1)} collective-permute-done((bf16[128,1152]{1,0:T(8,128)(2,1)S(1)}, bf16[128,1152]{1,0:T(8,128)(2,1)S(1)}, u32[]{:S(2)}, u32[]{:S(2)}) %collective-permute-start.13) | collective-permute-done | bytes 294944 | tf_op jit(solution)/shard_map/ppermute | solution.py:20
  301.1 1.4 collective-permute-start.15
  302.6 6.7 collective-permute-done.17
  310.4 3.8 collective-permute-done.15
  314.3 4.3 convolution_convert_fusion.2
  318.6 8.4 %multiply_convert_fusion = (bf16[512,1728]{0,1:T(8,128)(2,1)S(1)}, bf16[512,1728]{0,1:T(8,128)(2,1)S(1)}) fusion(f32[512,1728]{0,1:T(8,128)S(1)} %copy-done.77, f32[512,1728]{0,1:T(8,128)} %get-tuple-element.185, bf16[1728,1152]{0,1:T(8,128)(2,1)S(1)} %copy-done.67, bf16[128,1152]{1,0:T(8,128)(2,1)S(1)} %collective-permute-done.17, ...), kind=kOutput, calls=%fused_computation.20 | convolution fusion | flops 2064384000 | bytes 15777792 | tf_op jit(solution)/shard_map/ld,fd->lf/dot_general | solution.py:213
  327.1 2.6 fusion.1
  329.7 5.4 convolution_convert_fusion.1
  335.1 5.3 convolution_convert_fusion
  340.4 3.7 fusion.13
  344.1 6.5 copy.60
  350.7 6.5 copy.62
  357.2 2.2 fusion.94
  359.4 1.9 collective-permute-start.20
  361.2 1.4 collective-permute-start.19
  362.7 6.5 copy.64
  369.2 7.4 %collective-permute-done.19 = bf16[128,1152]{1,0:T(8,128)(2,1)} collective-permute-done((bf16[128,1152]{1,0:T(8,128)(2,1)}, bf16[128,1152]{1,0:T(8,128)(2,1)}, u32[]{:S(2)}, u32[]{:S(2)}) %collective-permute-start.19) | collective-permute-done | bytes 294944 | tf_op jit(solution)/shard_map/ppermute | solution.py:20
  376.6 1.6 multiply_reduce_fusion.1
  378.9 1.9 multiply_reduce_fusion.2
  383.5 4.9 collective-permute-done.21
  388.4 6.6 collective-permute-done.22
  403.9 13.7 %collective-permute-done.24 = bf16[512,256]{1,0:T(8,128)(2,1)S(1)} collective-permute-done((bf16[512,256]{1,0:T(8,128)(2,1)S(1)}, bf16[512,256]{1,0:T(8,128)(2,1)S(1)}, u32[]{:S(2)}, u32[]{:S(2)}) %collective-permute-start.24) | collective-permute-done | bytes 262176 | tf_op jit(solution)/shard_map/ppermute | solution.py:15
  433.4 2.1 collective-permute-done.27
  436.5 2.5 fusion.33
  439.1 1.4 stack.61
  440.5 1.6 fusion.14
  442.1 4.6 reduce-scatter.13.cloned.1.call-done
  446.7 2.3 copy.61
  449.0 89.0 %reduce-scatter.15.cloned.1.call-done = bf16[144,1728]{1,0:T(8,128)(2,1)} async-done(((bf16[1152,1728]{1,0:T(8,128)(2,1)}), bf16[144,1728]{1,0:T(8,128)(2,1)}) %reduce-scatter.15.cloned.1.call-update) | async-done | bytes 497680
  538.0 2.3 copy.63
  540.2 88.7 %reduce-scatter.17.cloned.1.call-done = bf16[144,1728]{1,0:T(8,128)(2,1)} async-done(((bf16[1152,1728]{1,0:T(8,128)(2,1)}), bf16[144,1728]{1,0:T(8,128)(2,1)}) %reduce-scatter.17.cloned.1.call-update) | async-done | bytes 497680
  628.9 2.3 copy.65
  631.2 3.3 copy.66
  637.2 2.2 copy.55
  640.7 1.5 copy.56
  642.2 62.7 %reduce-scatter.19.cloned.1.call-done = bf16[144,1152]{1,0:T(8,128)(2,1)} async-done(((bf16[1152,1152]{1,0:T(8,128)(2,1)}), bf16[144,1152]{1,0:T(8,128)(2,1)}) %reduce-scatter.19.cloned.1.call-update) | async-done | bytes 331792
  706.1 1.5 collective-permute-start.30
  710.5 2.7 collective-permute-done.31
  713.1 9.9 %collective-permute-done.30 = bf16[144,640]{0,1:T(8,128)(2,1)S(1)} collective-permute-done((bf16[144,640]{0,1:T(8,128)(2,1)S(1)}, bf16[144,640]{0,1:T(8,128)(2,1)S(1)}, u32[]{:S(2)}, u32[]{:S(2)}) %collective-permute-start.30) | collective-permute-done | bytes 184352 | tf_op jit(solution)/shard_map/ppermute | solution.py:20
  (320 shorter events, 61.9 us)
Async XLA Ops:
  7.2 63.9 %all-gather.4.cloned.1.call-start = ((), (), s32[]{:S(2)}) async-start(), calls=%async_computation.4 | async-start | bytes 2985984 | tf_op jit(solution)/shard_map/all_gather | solution.py:131
  13.2 191.2 %all-gather.6.cloned.1.call-start = ((), (), s32[]{:S(2)}) async-start(), calls=%async_computation.5 | async-start | bytes 9289728 | tf_op jit(solution)/shard_map/all_gather | solution.py:132
  13.9 263.5 %all-gather.8.cloned.1.call-start = ((), (), s32[]{:S(2)}) async-start(), calls=%async_computation.6 | async-start | bytes 4644864 | tf_op jit(solution)/shard_map/all_gather | solution.py:133
  14.1 59.7 %copy-start.61 = (f32[128]{0:T(128)}, f32[128]{0:T(128)S(1)}, u32[]{:S(2)}) copy-start(f32[128]{0:T(128)S(1)} %fusion.39) | copy-start | bytes 1540
  14.2 59.8 %copy-start.53 = (f32[128]{0:T(128)}, f32[128]{0:T(128)S(1)}, u32[]{:S(2)}) copy-start(f32[128]{0:T(128)S(1)} %fusion.79) | copy-start | bytes 1540
  74.1 6.2 collective-permute-start.1
  74.2 372.5 %reduce-scatter.13.cloned.1.call-start = ((), (), s32[]{:S(2)}) async-start(), calls=%async_computation.7 | async-start | bytes 4644864
  74.5 19.0 %copy-start.40 = (f32[512]{0:T(512)}, f32[512]{0:T(512)S(1)}, u32[]{:S(2)}) copy-start(f32[512]{0:T(512)S(1)} %convert_element_type.189) | copy-start | bytes 6148
  74.5 15.0 %collective-permute-start.2 = (bf16[128,1152]{1,0:T(8,128)(2,1)S(1)}, bf16[128,1152]{1,0:T(8,128)(2,1)S(1)}, u32[]{:S(2)}, u32[]{:S(2)}) collective-permute-start(bf16[128,1152]{1,0:T(8,128)(2,1)S(1)} %get-tuple-element.141), channel_id=1, source_target_pairs={{0,2},{1,3},{2,0},{3,1},{4,6},{5,7},{6,4},{7,5},{8,10},{9,11},{10,... | collective-permute-start | bytes 884744 | tf_op jit(solution)/shard_map/ppermute | solution.py:20
  76.0 17.5 %copy-start.58 = (f32[128]{0:T(128)}, f32[128]{0:T(128)S(1)}, u32[]{:S(2)}) copy-start(f32[128]{0:T(128)S(1)} %multiply_power_fusion) | copy-start | bytes 1540
  76.0 13.8 %collective-permute-start.3 = (bf16[128,1152]{1,0:T(8,128)(2,1)S(1)}, bf16[128,1152]{1,0:T(8,128)(2,1)S(1)}, u32[]{:S(2)}, u32[]{:S(2)}) collective-permute-start(bf16[128,1152]{1,0:T(8,128)(2,1)S(1)} %get-tuple-element.141), channel_id=1, source_target_pairs={{0,1},{1,2},{2,3},{3,0},{4,5},{5,6},{6,7},{7,4},{8,9},{9,10},{10,1... | collective-permute-start | bytes 884744 | tf_op jit(solution)/shard_map/ppermute | solution.py:20
  76.3 16.9 %copy-start.42 = (f32[256]{0:T(256)}, f32[256]{0:T(256)S(1)}, u32[]{:S(2)}) copy-start(f32[256]{0:T(256)S(1)} %mul.547) | copy-start | bytes 3076
  76.5 16.8 %copy-start.44 = (f32[256]{0:T(256)}, f32[256]{0:T(256)S(1)}, u32[]{:S(2)}) copy-start(f32[256]{0:T(256)S(1)} %mul.562) | copy-start | bytes 3076
  94.8 19.3 %copy-start.16 = (bf16[512,128]{1,0:T(8,128)(2,1)}, bf16[512,128]{1,0:T(8,128)(2,1)S(1)}, u32[]{:S(2)}) copy-start(bf16[512,128]{1,0:T(8,128)(2,1)S(1)} %get-tuple-element.180) | copy-start | bytes 393220
  94.8 19.3 %copy-start.18 = (bf16[512,128]{1,0:T(8,128)(2,1)}, bf16[512,128]{1,0:T(8,128)(2,1)S(1)}, u32[]{:S(2)}) copy-start(bf16[512,128]{1,0:T(8,128)(2,1)S(1)} %get-tuple-element.181) | copy-start | bytes 393220
  94.8 19.3 %copy-start.27 = (bf16[512,128]{1,0:T(8,128)(2,1)}, bf16[512,128]{1,0:T(8,128)(2,1)S(1)}, u32[]{:S(2)}) copy-start(bf16[512,128]{1,0:T(8,128)(2,1)S(1)} %get-tuple-element.166) | copy-start | bytes 393220
  94.8 19.3 %copy-start.29 = (bf16[512,128]{1,0:T(8,128)(2,1)}, bf16[512,128]{1,0:T(8,128)(2,1)S(1)}, u32[]{:S(2)}) copy-start(bf16[512,128]{1,0:T(8,128)(2,1)S(1)} %get-tuple-element.167) | copy-start | bytes 393220
  94.9 18.2 %collective-permute-start.4 = (bf16[512,256]{1,0:T(8,128)(2,1)S(1)}, bf16[512,256]{1,0:T(8,128)(2,1)S(1)}, u32[]{:S(2)}, u32[]{:S(2)}) collective-permute-start(bf16[512,256]{1,0:T(8,128)(2,1)S(1)} %pad_maximum_fusion.9), channel_id=1, source_target_pairs={{0,4},{4,8},{8,12},{12,16},{16,20},{20,24},{24,28},{1,5},{5,9},{9,... | collective-permute-start | bytes 786440 | tf_op jit(solution)/shard_map/ppermute | solution.py:15
  97.4 5.6 collective-permute-start
  103.1 13.9 %collective-permute-start.5 = (bf16[512,256]{1,0:T(8,128)(2,1)S(1)}, bf16[512,256]{1,0:T(8,128)(2,1)S(1)}, u32[]{:S(2)}, u32[]{:S(2)}) collective-permute-start(bf16[512,256]{1,0:T(8,128)(2,1)S(1)} %slice.321), channel_id=1, source_target_pairs={{0,4},{4,8},{8,12},{12,16},{16,20},{20,24},{24,28},{1,5},{5,9},{9,... | collective-permute-start | bytes 786440 | tf_op jit(solution)/shard_map/ppermute | solution.py:15
  117.7 16.5 %copy-start.14 = (bf16[512,256]{1,0:T(8,128)(2,1)}, bf16[512,256]{1,0:T(8,128)(2,1)S(1)}, u32[]{:S(2)}) copy-start(bf16[512,256]{1,0:T(8,128)(2,1)S(1)} %convolution_convert_fusion.9) | copy-start | bytes 786436
  119.4 15.6 %copy-start.3 = (bf16[128,1152]{1,0:T(8,128)(2,1)S(1)}, bf16[128,1152]{1,0:T(8,128)(2,1)}, u32[]{:S(2)}) copy-start(bf16[128,1152]{1,0:T(8,128)(2,1)} %param.23) | copy-start | bytes 884740
  119.4 15.9 %copy-start.26 = (f32[1152]{0:T(1024)S(1)}, f32[1152]{0:T(1024)}, u32[]{:S(2)}) copy-start(f32[1152]{0:T(1024)} %get-tuple-element.125) | copy-start | bytes 13828
  119.5 7.0 collective-permute-start.8
  119.6 14.6 %collective-permute-start.7 = (bf16[128,1152]{1,0:T(8,128)(2,1)S(1)}, bf16[128,1152]{1,0:T(8,128)(2,1)S(1)}, u32[]{:S(2)}, u32[]{:S(2)}) collective-permute-start(bf16[128,1152]{1,0:T(8,128)(2,1)S(1)} %get-tuple-element.159), channel_id=1, source_target_pairs={{0,2},{1,3},{2,0},{3,1},{4,6},{5,7},{6,4},{7,5},{8,10},{9,11},{10,... | collective-permute-start | bytes 884744 | tf_op jit(solution)/shard_map/ppermute | solution.py:20
  120.6 14.1 %collective-permute-start.6 = (bf16[128,1152]{1,0:T(8,128)(2,1)S(1)}, bf16[128,1152]{1,0:T(8,128)(2,1)S(1)}, u32[]{:S(2)}, u32[]{:S(2)}) collective-permute-start(bf16[128,1152]{1,0:T(8,128)(2,1)S(1)} %get-tuple-element.157), channel_id=1, source_target_pairs={{0,1},{1,2},{2,3},{3,0},{4,5},{5,6},{6,7},{7,4},{8,9},{9,10},{10,1... | collective-permute-start | bytes 884744 | tf_op jit(solution)/shard_map/ppermute | solution.py:20
  135.5 8.8 %collective-permute-start.11 = (bf16[128,1152]{1,0:T(8,128)(2,1)S(1)}, bf16[128,1152]{1,0:T(8,128)(2,1)S(1)}, u32[]{:S(2)}, u32[]{:S(2)}) collective-permute-start(bf16[128,1152]{1,0:T(8,128)(2,1)S(1)} %multiply_convert_fusion.3), channel_id=1, source_target_pairs={{0,1},{1,2},{2,3},{3,0},{4,5},{5,6},{6,7},{7,4},{8,9},{9,10},{10,1... | collective-permute-start | bytes 884744 | tf_op jit(solution)/shard_map/ppermute | solution.py:20
  135.5 9.9 %collective-permute-start.10 = (bf16[128,1152]{1,0:T(8,128)(2,1)S(1)}, bf16[128,1152]{1,0:T(8,128)(2,1)S(1)}, u32[]{:S(2)}, u32[]{:S(2)}) collective-permute-start(bf16[128,1152]{1,0:T(8,128)(2,1)S(1)} %multiply_convert_fusion.3), channel_id=1, source_target_pairs={{0,2},{1,3},{2,0},{3,1},{4,6},{5,7},{6,4},{7,5},{8,10},{9,11},{10,... | collective-permute-start | bytes 884744 | tf_op jit(solution)/shard_map/ppermute | solution.py:20
  136.7 13.1 %collective-permute-start.9 = (bf16[128,1152]{1,0:T(8,128)(2,1)S(1)}, bf16[128,1152]{1,0:T(8,128)(2,1)}, u32[]{:S(2)}, u32[]{:S(2)}) collective-permute-start(bf16[128,1152]{1,0:T(8,128)(2,1)S(1)} %multiply_convert_fusion.3), channel_id=1, source_target_pairs={{0,3},{1,0},{2,1},{3,2},{4,7},{5,4},{6,5},{7,6},{8,11},{9,8},{10,9... | collective-permute-start | bytes 884744 | tf_op jit(solution)/shard_map/ppermute | solution.py:20
  282.7 16.1 %copy-start.9 = (bf16[128,1152]{1,0:T(8,128)(2,1)S(1)}, bf16[128,1152]{1,0:T(8,128)(2,1)}, u32[]{:S(2)}) copy-start(bf16[128,1152]{1,0:T(8,128)(2,1)} %param.37) | copy-start | bytes 884740
  282.7 16.1 %copy-start.31 = (f32[1152]{0:T(1024)S(1)}, f32[1152]{0:T(1024)}, u32[]{:S(2)}) copy-start(f32[1152]{0:T(1024)} %get-tuple-element.124) | copy-start | bytes 13828
  282.8 6.4 collective-permute-start.14
  282.9 15.5 %collective-permute-start.13 = (bf16[128,1152]{1,0:T(8,128)(2,1)S(1)}, bf16[128,1152]{1,0:T(8,128)(2,1)S(1)}, u32[]{:S(2)}, u32[]{:S(2)}) collective-permute-start(bf16[128,1152]{1,0:T(8,128)(2,1)S(1)} %get-tuple-element.156), channel_id=1, source_target_pairs={{0,2},{1,3},{2,0},{3,1},{4,6},{5,7},{6,4},{7,5},{8,10},{9,11},{10,... | collective-permute-start | bytes 884744 | tf_op jit(solution)/shard_map/ppermute | solution.py:20
  284.4 29.9 %copy-start.78 = (bf16[512,1728]{0,1:T(8,128)(2,1)S(1)}, bf16[512,1728]{0,1:T(8,128)(2,1)}, u32[]{:S(2)}) copy-start(bf16[512,1728]{0,1:T(8,128)(2,1)} %get-tuple-element.184) | copy-start | bytes 5308420
  284.4 14.1 %collective-permute-start.12 = (bf16[128,1152]{1,0:T(8,128)(2,1)S(1)}, bf16[128,1152]{1,0:T(8,128)(2,1)S(1)}, u32[]{:S(2)}, u32[]{:S(2)}) collective-permute-start(bf16[128,1152]{1,0:T(8,128)(2,1)S(1)} %get-tuple-element.154), channel_id=1, source_target_pairs={{0,1},{1,2},{2,3},{3,0},{4,5},{5,6},{6,7},{7,4},{8,9},{9,10},{10,1... | collective-permute-start | bytes 884744 | tf_op jit(solution)/shard_map/ppermute | solution.py:20
  300.5 18.1 %copy-start.67 = (bf16[1728,1152]{0,1:T(8,128)(2,1)S(1)}, bf16[1728,1152]{0,1:T(8,128)(2,1)}, u32[]{:S(2)}) copy-start(bf16[1728,1152]{0,1:T(8,128)(2,1)} %all-gather.8.cloned.1.call-done) | copy-start | bytes 11943940
  300.5 18.1 %copy-start.77 = (f32[512,1728]{0,1:T(8,128)S(1)}, f32[512,1728]{0,1:T(8,128)}, u32[]{:S(2)}) copy-start(f32[512,1728]{0,1:T(8,128)} %copy-done.76) | copy-start | bytes 10616836
  300.5 8.8 %collective-permute-start.17 = (bf16[128,1152]{1,0:T(8,128)(2,1)S(1)}, bf16[128,1152]{1,0:T(8,128)(2,1)S(1)}, u32[]{:S(2)}, u32[]{:S(2)}) collective-permute-start(bf16[128,1152]{1,0:T(8,128)(2,1)S(1)} %get-tuple-element.160), channel_id=1, source_target_pairs={{0,1},{1,2},{2,3},{3,0},{4,5},{5,6},{6,7},{7,4},{8,9},{9,10},{10,1... | collective-permute-start | bytes 884744 | tf_op jit(solution)/shard_map/ppermute | solution.py:20
  300.6 9.9 %collective-permute-start.16 = (bf16[128,1152]{1,0:T(8,128)(2,1)S(1)}, bf16[128,1152]{1,0:T(8,128)(2,1)S(1)}, u32[]{:S(2)}, u32[]{:S(2)}) collective-permute-start(bf16[128,1152]{1,0:T(8,128)(2,1)S(1)} %get-tuple-element.160), channel_id=1, source_target_pairs={{0,2},{1,3},{2,0},{3,1},{4,6},{5,7},{6,4},{7,5},{8,10},{9,11},{10,... | collective-permute-start | bytes 884744 | tf_op jit(solution)/shard_map/ppermute | solution.py:20
  301.1 13.1 %collective-permute-start.15 = (bf16[128,1152]{1,0:T(8,128)(2,1)S(1)}, bf16[128,1152]{1,0:T(8,128)(2,1)S(1)}, u32[]{:S(2)}, u32[]{:S(2)}) collective-permute-start(bf16[128,1152]{1,0:T(8,128)(2,1)S(1)} %get-tuple-element.160), channel_id=1, source_target_pairs={{0,3},{1,0},{2,1},{3,2},{4,7},{5,4},{6,5},{7,6},{8,11},{9,8},{10,9... | collective-permute-start | bytes 884744 | tf_op jit(solution)/shard_map/ppermute | solution.py:20
  350.6 187.4 %reduce-scatter.15.cloned.1.call-start = ((), (), s32[]{:S(2)}) async-start(), calls=%async_computation.8 | async-start | bytes 4644864
  357.2 271.7 %reduce-scatter.17.cloned.1.call-start = ((), (), s32[]{:S(2)}) async-start(), calls=%async_computation.9 | async-start | bytes 4644864
  359.4 9.9 %collective-permute-start.20 = (bf16[128,1152]{1,0:T(8,128)(2,1)}, bf16[128,1152]{1,0:T(8,128)(2,1)}, u32[]{:S(2)}, u32[]{:S(2)}) collective-permute-start(bf16[128,1152]{1,0:T(8,128)(2,1)} %get-tuple-element.152), channel_id=1, source_target_pairs={{0,3},{1,0},{2,1},{3,2},{4,7},{5,4},{6,5},{7,6},{8,11},{9,8},{10,9... | collective-permute-start | bytes 884744 | tf_op jit(solution)/shard_map/ppermute | solution.py:20
  361.2 15.4 %collective-permute-start.19 = (bf16[128,1152]{1,0:T(8,128)(2,1)}, bf16[128,1152]{1,0:T(8,128)(2,1)}, u32[]{:S(2)}, u32[]{:S(2)}) collective-permute-start(bf16[128,1152]{1,0:T(8,128)(2,1)} %get-tuple-element.153), channel_id=1, source_target_pairs={{0,2},{1,3},{2,0},{3,1},{4,6},{5,7},{6,4},{7,5},{8,10},{9,11},{10,... | collective-permute-start | bytes 884744 | tf_op jit(solution)/shard_map/ppermute | solution.py:20
  362.7 14.0 %collective-permute-start.18 = (bf16[128,1152]{1,0:T(8,128)(2,1)}, bf16[128,1152]{1,0:T(8,128)(2,1)}, u32[]{:S(2)}, u32[]{:S(2)}) collective-permute-start(bf16[128,1152]{1,0:T(8,128)(2,1)} %get-tuple-element.151), channel_id=1, source_target_pairs={{0,1},{1,2},{2,3},{3,0},{4,5},{5,6},{6,7},{7,4},{8,9},{9,10},{10,1... | collective-permute-start | bytes 884744 | tf_op jit(solution)/shard_map/ppermute | solution.py:20
  369.2 335.7 %reduce-scatter.19.cloned.1.call-start = ((), (), s32[]{:S(2)}) async-start(), calls=%async_computation.10 | async-start | bytes 2985984
  380.7 15.3 %copy-start.5 = (f32[128,1152]{1,0:T(8,128)}, f32[128,1152]{1,0:T(8,128)S(1)}, u32[]{:S(2)}) copy-start(f32[128,1152]{1,0:T(8,128)S(1)} %get-tuple-element.133) | copy-start | bytes 1769476
  380.8 15.2 %copy-start.23 = (bf16[1152,1152]{1,0:T(8,128)(2,1)S(1)}, bf16[1152,1152]{1,0:T(8,128)(2,1)}, u32[]{:S(2)}) copy-start(bf16[1152,1152]{1,0:T(8,128)(2,1)} %all-gather.4.cloned.1.call-done) | copy-start | bytes 7962628
  381.1 7.3 collective-permute-start.21
  381.2 13.8 %collective-permute-start.22 = (bf16[128,1152]{1,0:T(8,128)(2,1)S(1)}, bf16[128,1152]{1,0:T(8,128)(2,1)S(1)}, u32[]{:S(2)}, u32[]{:S(2)}) collective-permute-start(bf16[128,1152]{1,0:T(8,128)(2,1)S(1)} %get-tuple-element.132), channel_id=1, source_target_pairs={{0,2},{1,3},{2,0},{3,1},{4,6},{5,7},{6,4},{7,5},{8,10},{9,11},{10,... | collective-permute-start | bytes 884744 | tf_op jit(solution)/shard_map/ppermute | solution.py:20
  381.9 14.1 %collective-permute-start.23 = (bf16[128,1152]{1,0:T(8,128)(2,1)S(1)}, bf16[128,1152]{1,0:T(8,128)(2,1)S(1)}, u32[]{:S(2)}, u32[]{:S(2)}) collective-permute-start(bf16[128,1152]{1,0:T(8,128)(2,1)S(1)} %get-tuple-element.132), channel_id=1, source_target_pairs={{0,1},{1,2},{2,3},{3,0},{4,5},{5,6},{6,7},{7,4},{8,9},{9,10},{10,1... | collective-permute-start | bytes 884744 | tf_op jit(solution)/shard_map/ppermute | solution.py:20
  397.2 22.6 %collective-permute-start.25 = (bf16[512,256]{1,0:T(8,128)(2,1)S(1)}, bf16[512,256]{1,0:T(8,128)(2,1)S(1)}, u32[]{:S(2)}, u32[]{:S(2)}) collective-permute-start(bf16[512,256]{1,0:T(8,128)(2,1)S(1)} %slice.319), channel_id=1, source_target_pairs={{4,0},{8,4},{12,8},{16,12},{20,16},{24,20},{28,24},{5,1},{9,5},{13... | collective-permute-start | bytes 786440 | tf_op jit(solution)/shard_map/ppermute | solution.py:15
  400.6 16.9 %collective-permute-start.24 = (bf16[512,256]{1,0:T(8,128)(2,1)S(1)}, bf16[512,256]{1,0:T(8,128)(2,1)S(1)}, u32[]{:S(2)}, u32[]{:S(2)}) collective-permute-start(bf16[512,256]{1,0:T(8,128)(2,1)S(1)} %slice.320), channel_id=1, source_target_pairs={{4,0},{8,4},{12,8},{16,12},{20,16},{24,20},{28,24},{5,1},{9,5},{13... | collective-permute-start | bytes 786440 | tf_op jit(solution)/shard_map/ppermute | solution.py:15
  403.8 15.1 %copy-start.1 = (f32[512,768]{1,0:T(8,128)S(1)}, f32[512,768]{1,0:T(8,128)}, u32[]{:S(2)}) copy-start(f32[512,768]{1,0:T(8,128)} %copy-done) | copy-start | bytes 4718596
  403.8 15.1 %copy-start.33 = (f32[512]{0:T(512)S(1)}, f32[512]{0:T(512)}, u32[]{:S(2)}) copy-start(f32[512]{0:T(512)} %copy-done.32) | copy-start | bytes 6148
  403.8 15.1 %copy-start.35 = (f32[512]{0:T(512)S(1)}, f32[512]{0:T(512)}, u32[]{:S(2)}) copy-start(f32[512]{0:T(512)} %copy-done.34) | copy-start | bytes 6148
  403.8 15.1 %copy-start.43 = (f32[256]{0:T(256)S(1)}, f32[256]{0:T(256)}, u32[]{:S(2)}) copy-start(f32[256]{0:T(256)} %copy-done.42) | copy-start | bytes 3076
  421.6 11.8 %collective-permute-start.28 = (bf16[128,1152]{1,0:T(8,128)(2,1)S(1)}, bf16[128,1152]{1,0:T(8,128)(2,1)S(1)}, u32[]{:S(2)}, u32[]{:S(2)}) collective-permute-start(bf16[128,1152]{1,0:T(8,128)(2,1)S(1)} %get-tuple-element.149), channel_id=1, source_target_pairs={{0,3},{1,0},{2,1},{3,2},{4,7},{5,4},{6,5},{7,6},{8,11},{9,8},{10,9... | collective-permute-start | bytes 884744 | tf_op jit(solution)/shard_map/ppermute | solution.py:20
  421.7 13.8 %collective-permute-start.27 = (bf16[128,1152]{1,0:T(8,128)(2,1)S(1)}, bf16[128,1152]{1,0:T(8,128)(2,1)S(1)}, u32[]{:S(2)}, u32[]{:S(2)}) collective-permute-start(bf16[128,1152]{1,0:T(8,128)(2,1)S(1)} %get-tuple-element.150), channel_id=1, source_target_pairs={{0,2},{1,3},{2,0},{3,1},{4,6},{5,7},{6,4},{7,5},{8,10},{9,11},{10,... | collective-permute-start | bytes 884744 | tf_op jit(solution)/shard_map/ppermute | solution.py:20
  422.3 14.2 %collective-permute-start.26 = (bf16[128,1152]{1,0:T(8,128)(2,1)S(1)}, bf16[128,1152]{1,0:T(8,128)(2,1)}, u32[]{:S(2)}, u32[]{:S(2)}) collective-permute-start(bf16[128,1152]{1,0:T(8,128)(2,1)S(1)} %get-tuple-element.148), channel_id=1, source_target_pairs={{0,1},{1,2},{2,3},{3,0},{4,5},{5,6},{6,7},{7,4},{8,9},{9,10},{10,1... | collective-permute-start | bytes 884744 | tf_op jit(solution)/shard_map/ppermute | solution.py:20
  425.3 15.1 %slice-start = ((bf16[1152,768]{0,1:T(8,128)(2,1)}), bf16[1152,256]{0,1:T(8,128)(2,1)S(1)}, s32[]{:S(2)}) async-start(bf16[1152,768]{0,1:T(8,128)(2,1)} %copy-done.10), calls=%async_computation.11 | async-start | bytes 1179648 | tf_op jit(solution)/shard_map/slice | solution.py:316
  706.0 7.1 collective-permute-start.31
  706.1 16.9 %collective-permute-start.30 = (bf16[144,640]{0,1:T(8,128)(2,1)S(1)}, bf16[144,640]{0,1:T(8,128)(2,1)S(1)}, u32[]{:S(2)}, u32[]{:S(2)}) collective-permute-start(bf16[144,640]{0,1:T(8,128)(2,1)S(1)} %copy.69), channel_id=1, source_target_pairs={{0,2},{1,3},{2,0},{3,1},{4,6},{5,7},{6,4},{7,5},{8,10},{9,11},{10,... | collective-permute-start | bytes 552968 | tf_op jit(solution)/shard_map/ppermute | solution.py:20
  707.6 15.5 %collective-permute-start.29 = (bf16[144,640]{0,1:T(8,128)(2,1)S(1)}, bf16[144,640]{0,1:T(8,128)(2,1)S(1)}, u32[]{:S(2)}, u32[]{:S(2)}) collective-permute-start(bf16[144,640]{0,1:T(8,128)(2,1)S(1)} %copy.69), channel_id=1, source_target_pairs={{0,1},{1,2},{2,3},{3,0},{4,5},{5,6},{6,7},{7,4},{8,9},{9,10},{10,1... | collective-permute-start | bytes 552968 | tf_op jit(solution)/shard_map/ppermute | solution.py:20
  (57 other events, 248.7 us)
Sparse Core Ops, SparseCore 0:
  13.3 57.7 all-gather.3
  73.3 131.1 all-gather.5
  206.6 70.7 all-gather.7
  350.7 95.9 reduce-scatter.12
  450.5 87.4 reduce-scatter.14
  541.4 87.4 reduce-scatter.16
  634.6 70.2 reduce-scatter.18
where the time goes:
time: 740 us; the launch traced here: 732 us
  waiting for transfers between devices  533 us (72%)
  local copies, waits for them, and re-layouts  65.2 us (9%)
  matrix products  59.8 us (8%)
  starting transfers between devices  36.2 us (5%)
  other arithmetic  22.5 us (3%)
  between operations  15.8 us (2%)
    unnamed x11, waiting for transfers between devices  246 us
    ppermute x27, waiting for transfers between devices, shifted(): lax.ppermute(value, axis, [(i, (i + shift) % count) for i in range(count)])  99.2 us
    all_gather x1, waiting for transfers between devices, local(): down_full = lax.all_gather(down_weight, 'dp', axis=1, tiled=True)  59.2 us
    all_gather x1, waiting for transfers between devices, local(): packed_full = lax.all_gather(packed, 'dp', axis=0, tiled=True)  56.9 us
    all_gather x1, waiting for transfers between devices, local(): gate_up_full = lax.all_gather(gate_up_weight, 'dp', axis=1, tiled=True)  54.7 us
    unnamed x175, local copies, waits for them, and re-layouts  34.6 us
    ppermute x5, starting transfers between devices, from_behind(): lax.ppermute(value, axis, [(source, source + steps) for source in range(l...  19.4 us
    ppermute x5, waiting for transfers between devices, from_behind(): lax.ppermute(value, axis, [(source, source + steps) for source in range(l...  17.3 us
  transfers between devices with their start and end apart: 39, of which 34 were waited for; matrix products, arithmetic and copies ran while one was open for 11% of the time, Pallas kernels for 0%

commit v1 on v0

--- a/solution.py
+++ b/solution.py
@@ -128,7 +128,13 @@
     )
     gain_columns = jnp.pad(gain_columns, ((0, 0), (0, 128 - gain_columns.shape[1])))
     packed = jnp.concatenate([q_weight, kv_weight, jnp.transpose(o_weight), gain_columns], axis=1)
-    packed_full = lax.all_gather(packed, "dp", axis=0, tiled=True)
+    devices = lax.axis_size("dp")
+    held, shards = (packed, [packed])
+    for _ in range(devices - 1):
+        held = lax.ppermute(held, "dp", [(i_2, (i_2 + 1) % devices) for i_2 in range(devices)])
+        shards.insert(0, held)
+    row_of_blocks = jnp.concatenate(shards, axis=0)
+    packed_full = jnp.roll(row_of_blocks, (lax.axis_index("dp") + 1) * packed.shape[0], axis=0)
     gate_up_full = lax.all_gather(gate_up_weight, "dp", axis=1, tiled=True)
     down_full = lax.all_gather(down_weight, "dp", axis=1, tiled=True)
     joint_weight = packed_full[:, : 3 * head_size]

time: 740 us -> 732 us (0.989)
  waiting for transfers between devices: 533 us -> 499 us
  matrix products: 59.8 us -> 71.2 us
  starting transfers between devices: 36.2 us -> 45.2 us
    ppermute x0 -> x7, waiting for transfers between devices: none -> 119 us  [local(): lax.ppermute(held, 'dp', [(i_2, (i_2 + 1) % devices) for i_2 in range(dev...]
    all_gather x1 -> x0, waiting for transfers between devices: 56.9 us -> none  [local(): packed_full = lax.all_gather(packed, 'dp', axis=0, tiled=True)]
    all_gather x1, waiting for transfers between devices: 54.7 us -> 0.01 us  [local(): gate_up_full = lax.all_gather(gate_up_weight, 'dp', axis=1, tiled=True)]
    all_gather x1, waiting for transfers between devices: 59.2 us -> 12.9 us  [local(): down_full = lax.all_gather(down_weight, 'dp', axis=1, tiled=True)]
    dot_general x1, matrix products: 8.38 us -> 16.7 us  [local(): jnp.einsum('ld,fd->lf', ff_grad_all, down_full, preferred_element_type=jn...]
    unnamed x175 -> x195, local copies, waits for them, and re-layouts: 34.6 us -> 38.7 us
    unnamed x11 -> x10, waiting for transfers between devices: 246 us -> 247 us
  transfers between devices with their start and end apart: 39 -> 45, of which waited for: 34 -> 39; matrix products, arithmetic and copies ran while one was open for 11% -> 13% of each run, Pallas kernels for 0% -> 0%
where the time goes in v1:
time: 732 us; the launch traced here: 723 us
  waiting for transfers between devices  499 us (68%)
  matrix products  71.2 us (10%)
  local copies, waits for them, and re-layouts  69 us (9%)
  starting transfers between devices  45.2 us (6%)
  other arithmetic  22 us (3%)
  between operations  16.1 us (2%)
    unnamed x10, waiting for transfers between devices  247 us
    ppermute x7, waiting for transfers between devices, local(): lax.ppermute(held, 'dp', [(i_2, (i_2 + 1) % devices) for i_2 in range(dev...  119 us
    ppermute x27, waiting for transfers between devices, shifted(): lax.ppermute(value, axis, [(i, (i + shift) % count) for i in range(count)])  99 us
    unnamed x195, local copies, waits for them, and re-layouts  38.7 us
    ppermute x5, starting transfers between devices, from_behind(): lax.ppermute(value, axis, [(source, source + steps) for source in range(l...  23.5 us
    ppermute x5, waiting for transfers between devices, from_behind(): lax.ppermute(value, axis, [(source, source + steps) for source in range(l...  22 us
    ppermute x27, starting transfers between devices, shifted(): lax.ppermute(value, axis, [(i, (i + shift) % count) for i in range(count)])  17.5 us
    dot_general x1, matrix products, local(): jnp.einsum('ld,fd->lf', ff_grad_all, down_full, preferred_element_type=jn...  16.7 us
  transfers between devices with their start and end apart: 45, of which 39 were waited for; matrix products, arithmetic and copies ran while one was open for 13% of the time, Pallas kernels for 0%

profile of v1, /device:TPU:0, one launch (start us, length us, event | category | flops | bytes accessed | tf_op | source)
XLA Modules:
  0.0 722.7 jit_solution(11633733469663234833)
XLA Ops:
  13.1 3.0 collective-permute-start.1
  16.1 11.0 %collective-permute-done.1 = bf16[144,1152]{1,0:T(8,128)(2,1)S(1)} collective-permute-done((bf16[144,1152]{1,0:T(8,128)(2,1)S(1)}, bf16[144,1152]{1,0:T(8,128)(2,1)S(1)}, u32[]{:S(2)}, u32[]{:S(2)}) %collective-permute-start.1) | collective-permute-done | bytes 331808 | tf_op jit(solution)/shard_map/ppermute | solution.py:134
  28.1 18.9 %collective-permute-done.2 = bf16[144,1152]{1,0:T(8,128)(2,1)S(1)} collective-permute-done((bf16[144,1152]{1,0:T(8,128)(2,1)S(1)}, bf16[144,1152]{1,0:T(8,128)(2,1)S(1)}, u32[]{:S(2)}, u32[]{:S(2)}) %collective-permute-start.2) | collective-permute-done | bytes 331808 | tf_op jit(solution)/shard_map/ppermute | solution.py:134
  47.0 19.5 %collective-permute-done.3 = bf16[144,1152]{1,0:T(8,128)(2,1)S(1)} collective-permute-done((bf16[144,1152]{1,0:T(8,128)(2,1)S(1)}, bf16[144,1152]{1,0:T(8,128)(2,1)S(1)}, u32[]{:S(2)}, u32[]{:S(2)}) %collective-permute-start.3) | collective-permute-done | bytes 331808 | tf_op jit(solution)/shard_map/ppermute | solution.py:134
  66.5 15.3 %collective-permute-done.4 = bf16[144,1152]{1,0:T(8,128)(2,1)S(1)} collective-permute-done((bf16[144,1152]{1,0:T(8,128)(2,1)S(1)}, bf16[144,1152]{1,0:T(8,128)(2,1)S(1)}, u32[]{:S(2)}, u32[]{:S(2)}) %collective-permute-start.4) | collective-permute-done | bytes 331808 | tf_op jit(solution)/shard_map/ppermute | solution.py:134
  81.8 17.5 %collective-permute-done.5 = bf16[144,1152]{1,0:T(8,128)(2,1)S(1)} collective-permute-done((bf16[144,1152]{1,0:T(8,128)(2,1)S(1)}, bf16[144,1152]{1,0:T(8,128)(2,1)S(1)}, u32[]{:S(2)}, u32[]{:S(2)}) %collective-permute-start.5) | collective-permute-done | bytes 331808 | tf_op jit(solution)/shard_map/ppermute | solution.py:134
  99.3 18.6 %collective-permute-done.6 = bf16[144,1152]{1,0:T(8,128)(2,1)S(1)} collective-permute-done((bf16[144,1152]{1,0:T(8,128)(2,1)S(1)}, bf16[144,1152]{1,0:T(8,128)(2,1)S(1)}, u32[]{:S(2)}, u32[]{:S(2)}) %collective-permute-start.6) | collective-permute-done | bytes 331808 | tf_op jit(solution)/shard_map/ppermute | solution.py:134
  119.1 18.0 %collective-permute-done.7 = bf16[144,1152]{1,0:T(8,128)(2,1)S(1)} collective-permute-done((bf16[144,1152]{1,0:T(8,128)(2,1)S(1)}, bf16[144,1152]{1,0:T(8,128)(2,1)S(1)}, u32[]{:S(2)}, u32[]{:S(2)}) %collective-permute-start.7) | collective-permute-done | bytes 331808 | tf_op jit(solution)/shard_map/ppermute | solution.py:134
  137.8 2.4 copy-done.26
  140.4 1.8 slice_reduce_fusion
  144.7 4.0 collective-permute-done.8
  148.7 9.1 %collective-permute-done.9 = bf16[128,1152]{1,0:T(8,128)(2,1)S(1)} collective-permute-done((bf16[128,1152]{1,0:T(8,128)(2,1)S(1)}, bf16[128,1152]{1,0:T(8,128)(2,1)S(1)}, u32[]{:S(2)}, u32[]{:S(2)}) %collective-permute-start.9) | collective-permute-done | bytes 294944 | tf_op jit(solution)/shard_map/ppermute | solution.py:20
  158.1 3.1 fusion.22
  164.9 13.2 %collective-permute-start = (bf16[512]{0:T(512)(128)(2,1)S(1)}, bf16[512]{0:T(512)(128)(2,1)S(1)}, u32[]{:S(2)}, u32[]{:S(2)}) collective-permute-start(bf16[512]{0:T(512)(128)(2,1)S(1)} %add_convert_fusion.1), channel_id=1, source_target_pairs={{0,4},{4,8},{8,12},{12,16},{16,20},{20,24},{24,28},{1,5},{5,9},{9,... | collective-permute-start | bytes 3080 | tf_op jit(solution)/shard_map/ppermute | solution.py:15
  179.4 6.4 collective-permute-start.12
  187.4 6.7 collective-permute-done.12
  194.8 1.8 convolution_convert_fusion.6
  196.8 1.6 collective-permute-start.14
  198.6 4.6 collective-permute-done.15
  203.1 9.3 %collective-permute-done.14 = bf16[128,1152]{1,0:T(8,128)(2,1)S(1)} collective-permute-done((bf16[128,1152]{1,0:T(8,128)(2,1)S(1)}, bf16[128,1152]{1,0:T(8,128)(2,1)S(1)}, u32[]{:S(2)}, u32[]{:S(2)}) %collective-permute-start.14) | collective-permute-done | bytes 294944 | tf_op jit(solution)/shard_map/ppermute | solution.py:20
  214.9 1.6 collective-permute-start.16
  216.5 6.4 collective-permute-done.18
  225.0 3.0 collective-permute-done.16
  228.0 5.2 fusion.2
  233.2 1.9 copy-done.79
  235.1 6.7 multiply_convert_fusion.1
  241.8 12.9 %all-gather.5.cloned.1.call-done = bf16[1728,1152]{0,1:T(8,128)(2,1)} async-done(((bf16[1728,144]{0,1:T(8,128)(2,1)}), bf16[1728,1152]{0,1:T(8,128)(2,1)}) %all-gather.5.cloned.1.call-update) | async-done | bytes 3981328 | tf_op jit(solution)/shard_map/all_gather | solution.py:139
  254.7 5.3 convolution_convert_fusion.5
  261.9 4.7 collective-permute-done.21
  266.6 9.1 %collective-permute-done.20 = bf16[128,1152]{1,0:T(8,128)(2,1)S(1)} collective-permute-done((bf16[128,1152]{1,0:T(8,128)(2,1)S(1)}, bf16[128,1152]{1,0:T(8,128)(2,1)S(1)}, u32[]{:S(2)}, u32[]{:S(2)}) %collective-permute-start.20) | collective-permute-done | bytes 294944 | tf_op jit(solution)/shard_map/ppermute | solution.py:20
  279.9 6.7 collective-permute-done.24
  287.8 3.9 collective-permute-done.22
  291.6 4.4 convolution_convert_fusion.2
  296.0 16.7 %multiply_convert_fusion = (bf16[512,1728]{0,1:T(8,128)(2,1)S(1)}, bf16[512,1728]{0,1:T(8,128)(2,1)S(1)}) fusion(f32[512,1728]{0,1:T(8,128)S(1)} %copy-done.80, f32[512,1728]{0,1:T(8,128)} %get-tuple-element.185, bf16[1728,1152]{0,1:T(8,128)(2,1)S(1)} %copy-done.70, bf16[128,1152]{1,0:T(8,128)(2,1)S(1)} %collective-permute-done.24, ...), kind=kOutput, calls=%fused_computation.20 | convolution fusion | flops 2064384000 | bytes 15777792 | tf_op jit(solution)/shard_map/ld,fd->lf/dot_general | solution.py:219
  312.8 2.6 fusion.1
  315.4 5.3 convolution_convert_fusion.1
  320.8 5.4 convolution_convert_fusion
  326.1 3.7 fusion.13
  329.9 6.5 copy.60
  336.4 6.4 copy.62
  342.9 2.1 fusion.96
  345.0 1.9 collective-permute-start.27
  348.4 6.4 copy.64
  354.9 7.4 %collective-permute-done.26 = bf16[128,1152]{1,0:T(8,128)(2,1)} collective-permute-done((bf16[128,1152]{1,0:T(8,128)(2,1)}, bf16[128,1152]{1,0:T(8,128)(2,1)}, u32[]{:S(2)}, u32[]{:S(2)}) %collective-permute-start.26) | collective-permute-done | bytes 294944 | tf_op jit(solution)/shard_map/ppermute | solution.py:20
  364.5 1.9 multiply_reduce_fusion.2
  369.1 5.1 collective-permute-done.28
  374.3 6.3 collective-permute-done.29
  381.6 1.7 convolution_convert_fusion.8
  390.7 13.9 %collective-permute-done.31 = bf16[512,256]{1,0:T(8,128)(2,1)S(1)} collective-permute-done((bf16[512,256]{1,0:T(8,128)(2,1)S(1)}, bf16[512,256]{1,0:T(8,128)(2,1)S(1)}, u32[]{:S(2)}, u32[]{:S(2)}) %collective-permute-start.31) | collective-permute-done | bytes 262176 | tf_op jit(solution)/shard_map/ppermute | solution.py:15
  407.3 2.8 convolution_convert_fusion.4
  422.8 2.6 collective-permute-done.34
  425.8 2.5 fusion.33
  429.8 1.7 fusion.14
  431.4 5.2 reduce-scatter.13.cloned.1.call-done
  436.6 2.3 copy.61
  438.9 88.8 %reduce-scatter.15.cloned.1.call-done = bf16[144,1728]{1,0:T(8,128)(2,1)} async-done(((bf16[1152,1728]{1,0:T(8,128)(2,1)}), bf16[144,1728]{1,0:T(8,128)(2,1)}) %reduce-scatter.15.cloned.1.call-update) | async-done | bytes 497680
  527.8 2.3 copy.63
  530.0 88.5 %reduce-scatter.17.cloned.1.call-done = bf16[144,1728]{1,0:T(8,128)(2,1)} async-done(((bf16[1152,1728]{1,0:T(8,128)(2,1)}), bf16[144,1728]{1,0:T(8,128)(2,1)}) %reduce-scatter.17.cloned.1.call-update) | async-done | bytes 497680
  618.5 2.3 copy.65
  620.8 3.3 copy.66
  626.8 2.2 copy.55
  631.8 63.2 %reduce-scatter.19.cloned.1.call-done = bf16[144,1152]{1,0:T(8,128)(2,1)} async-done(((bf16[1152,1152]{1,0:T(8,128)(2,1)}), bf16[144,1152]{1,0:T(8,128)(2,1)}) %reduce-scatter.19.cloned.1.call-update) | async-done | bytes 331792
  700.6 2.7 collective-permute-done.38
  703.3 9.8 %collective-permute-done.37 = bf16[144,640]{0,1:T(8,128)(2,1)S(1)} collective-permute-done((bf16[144,640]{0,1:T(8,128)(2,1)S(1)}, bf16[144,640]{0,1:T(8,128)(2,1)S(1)}, u32[]{:S(2)}, u32[]{:S(2)}) %collective-permute-start.37) | collective-permute-done | bytes 184352 | tf_op jit(solution)/shard_map/ppermute | solution.py:20
  (353 shorter events, 75.2 us)
Async XLA Ops:
  7.2 220.8 %all-gather.3.cloned.1.call-start = ((), (), s32[]{:S(2)}) async-start(), calls=%async_computation.4 | async-start | bytes 9289728 | tf_op jit(solution)/shard_map/all_gather | solution.py:138
  7.9 246.8 %all-gather.5.cloned.1.call-start = ((), (), s32[]{:S(2)}) async-start(), calls=%async_computation.5 | async-start | bytes 4644864 | tf_op jit(solution)/shard_map/all_gather | solution.py:139
  13.1 14.0 %collective-permute-start.1 = (bf16[144,1152]{1,0:T(8,128)(2,1)S(1)}, bf16[144,1152]{1,0:T(8,128)(2,1)S(1)}, u32[]{:S(2)}, u32[]{:S(2)}) collective-permute-start(bf16[144,1152]{1,0:T(8,128)(2,1)S(1)} %fusion.63), channel_id=1, source_target_pairs={{0,4},{4,8},{8,12},{12,16},{16,20},{20,24},{24,28},{28,0},{1,5},{5... | collective-permute-start | bytes 995336 | tf_op jit(solution)/shard_map/ppermute | solution.py:134
  27.2 19.8 %collective-permute-start.2 = (bf16[144,1152]{1,0:T(8,128)(2,1)S(1)}, bf16[144,1152]{1,0:T(8,128)(2,1)S(1)}, u32[]{:S(2)}, u32[]{:S(2)}) collective-permute-start(bf16[144,1152]{1,0:T(8,128)(2,1)S(1)} %collective-permute-done.1), channel_id=1, source_target_pairs={{0,4},{4,8},{8,12},{12,16},{16,20},{20,24},{24,28},{28,0},{1,5},{5... | collective-permute-start | bytes 995336 | tf_op jit(solution)/shard_map/ppermute | solution.py:134
  47.0 19.5 %collective-permute-start.3 = (bf16[144,1152]{1,0:T(8,128)(2,1)S(1)}, bf16[144,1152]{1,0:T(8,128)(2,1)S(1)}, u32[]{:S(2)}, u32[]{:S(2)}) collective-permute-start(bf16[144,1152]{1,0:T(8,128)(2,1)S(1)} %collective-permute-done.2), channel_id=1, source_target_pairs={{0,4},{4,8},{8,12},{12,16},{16,20},{20,24},{24,28},{28,0},{1,5},{5... | collective-permute-start | bytes 995336 | tf_op jit(solution)/shard_map/ppermute | solution.py:134
  66.5 15.3 %collective-permute-start.4 = (bf16[144,1152]{1,0:T(8,128)(2,1)S(1)}, bf16[144,1152]{1,0:T(8,128)(2,1)S(1)}, u32[]{:S(2)}, u32[]{:S(2)}) collective-permute-start(bf16[144,1152]{1,0:T(8,128)(2,1)S(1)} %collective-permute-done.3), channel_id=1, source_target_pairs={{0,4},{4,8},{8,12},{12,16},{16,20},{20,24},{24,28},{28,0},{1,5},{5... | collective-permute-start | bytes 995336 | tf_op jit(solution)/shard_map/ppermute | solution.py:134
  81.8 17.5 %collective-permute-start.5 = (bf16[144,1152]{1,0:T(8,128)(2,1)S(1)}, bf16[144,1152]{1,0:T(8,128)(2,1)S(1)}, u32[]{:S(2)}, u32[]{:S(2)}) collective-permute-start(bf16[144,1152]{1,0:T(8,128)(2,1)S(1)} %collective-permute-done.4), channel_id=1, source_target_pairs={{0,4},{4,8},{8,12},{12,16},{16,20},{20,24},{24,28},{28,0},{1,5},{5... | collective-permute-start | bytes 995336 | tf_op jit(solution)/shard_map/ppermute | solution.py:134
  99.3 18.6 %collective-permute-start.6 = (bf16[144,1152]{1,0:T(8,128)(2,1)S(1)}, bf16[144,1152]{1,0:T(8,128)(2,1)S(1)}, u32[]{:S(2)}, u32[]{:S(2)}) collective-permute-start(bf16[144,1152]{1,0:T(8,128)(2,1)S(1)} %collective-permute-done.5), channel_id=1, source_target_pairs={{0,4},{4,8},{8,12},{12,16},{16,20},{20,24},{24,28},{28,0},{1,5},{5... | collective-permute-start | bytes 995336 | tf_op jit(solution)/shard_map/ppermute | solution.py:134
  118.0 19.1 %collective-permute-start.7 = (bf16[144,1152]{1,0:T(8,128)(2,1)S(1)}, bf16[144,1152]{1,0:T(8,128)(2,1)S(1)}, u32[]{:S(2)}, u32[]{:S(2)}) collective-permute-start(bf16[144,1152]{1,0:T(8,128)(2,1)S(1)} %collective-permute-done.6), channel_id=1, source_target_pairs={{0,4},{4,8},{8,12},{12,16},{16,20},{20,24},{24,28},{28,0},{1,5},{5... | collective-permute-start | bytes 995336 | tf_op jit(solution)/shard_map/ppermute | solution.py:134
  119.1 18.4 %copy-start.64 = (f32[128]{0:T(128)}, f32[128]{0:T(128)S(1)}, u32[]{:S(2)}) copy-start(f32[128]{0:T(128)S(1)} %fusion.39) | copy-start | bytes 1540
  119.1 18.3 %copy-start.12 = (bf16[144,512]{1,0:T(8,128)(2,1)S(1)}, bf16[144,512]{1,0:T(8,128)(2,1)}, u32[]{:S(2)}) copy-start(bf16[144,512]{1,0:T(8,128)(2,1)} %param.27) | copy-start | bytes 442372
  119.1 18.3 %copy-start.17 = (bf16[256,144]{0,1:T(8,128)(2,1)S(1)}, bf16[256,144]{0,1:T(8,128)(2,1)}, u32[]{:S(2)}) copy-start(bf16[256,144]{0,1:T(8,128)(2,1)} %param.28) | copy-start | bytes 221188
  119.1 18.3 %copy-start.18 = (bf16[144,256]{1,0:T(8,128)(2,1)S(1)}, bf16[144,256]{1,0:T(8,128)(2,1)}, u32[]{:S(2)}) copy-start(bf16[144,256]{1,0:T(8,128)(2,1)} %param.26) | copy-start | bytes 221188
  119.1 23.1 %copy-start.56 = (f32[128]{0:T(128)}, f32[128]{0:T(128)S(1)}, u32[]{:S(2)}) copy-start(f32[128]{0:T(128)S(1)} %fusion.81) | copy-start | bytes 1540
  142.4 6.3 collective-permute-start.8
  142.5 294.1 %reduce-scatter.13.cloned.1.call-start = ((), (), s32[]{:S(2)}) async-start(), calls=%async_computation.6 | async-start | bytes 4644864
  142.6 19.6 %copy-start.43 = (f32[512]{0:T(512)}, f32[512]{0:T(512)S(1)}, u32[]{:S(2)}) copy-start(f32[512]{0:T(512)S(1)} %convert_element_type.189) | copy-start | bytes 6148
  142.6 15.2 %collective-permute-start.9 = (bf16[128,1152]{1,0:T(8,128)(2,1)S(1)}, bf16[128,1152]{1,0:T(8,128)(2,1)S(1)}, u32[]{:S(2)}, u32[]{:S(2)}) collective-permute-start(bf16[128,1152]{1,0:T(8,128)(2,1)S(1)} %get-tuple-element.141), channel_id=1, source_target_pairs={{0,2},{1,3},{2,0},{3,1},{4,6},{5,7},{6,4},{7,5},{8,10},{9,11},{10,... | collective-permute-start | bytes 884744 | tf_op jit(solution)/shard_map/ppermute | solution.py:20
  144.1 18.1 %copy-start.61 = (f32[128]{0:T(128)}, f32[128]{0:T(128)S(1)}, u32[]{:S(2)}) copy-start(f32[128]{0:T(128)S(1)} %multiply_power_fusion) | copy-start | bytes 1540
  144.1 14.0 %collective-permute-start.10 = (bf16[128,1152]{1,0:T(8,128)(2,1)S(1)}, bf16[128,1152]{1,0:T(8,128)(2,1)S(1)}, u32[]{:S(2)}, u32[]{:S(2)}) collective-permute-start(bf16[128,1152]{1,0:T(8,128)(2,1)S(1)} %get-tuple-element.141), channel_id=1, source_target_pairs={{0,1},{1,2},{2,3},{3,0},{4,5},{5,6},{6,7},{7,4},{8,9},{9,10},{10,1... | collective-permute-start | bytes 884744 | tf_op jit(solution)/shard_map/ppermute | solution.py:20
  161.3 18.1 %copy-start = (f32[512,768]{1,0:T(8,128)}, f32[512,768]{1,0:T(8,128)S(1)}, u32[]{:S(2)}) copy-start(f32[512,768]{1,0:T(8,128)S(1)} %fusion.22) | copy-start | bytes 4718596
  163.5 23.4 %copy-start.19 = (bf16[512,128]{1,0:T(8,128)(2,1)}, bf16[512,128]{1,0:T(8,128)(2,1)S(1)}, u32[]{:S(2)}) copy-start(bf16[512,128]{1,0:T(8,128)(2,1)S(1)} %get-tuple-element.180) | copy-start | bytes 393220
  163.5 23.4 %copy-start.21 = (bf16[512,128]{1,0:T(8,128)(2,1)}, bf16[512,128]{1,0:T(8,128)(2,1)S(1)}, u32[]{:S(2)}) copy-start(bf16[512,128]{1,0:T(8,128)(2,1)S(1)} %get-tuple-element.181) | copy-start | bytes 393220
  163.5 23.4 %copy-start.30 = (bf16[512,128]{1,0:T(8,128)(2,1)}, bf16[512,128]{1,0:T(8,128)(2,1)S(1)}, u32[]{:S(2)}) copy-start(bf16[512,128]{1,0:T(8,128)(2,1)S(1)} %get-tuple-element.166) | copy-start | bytes 393220
  163.5 23.4 %copy-start.32 = (bf16[512,128]{1,0:T(8,128)(2,1)}, bf16[512,128]{1,0:T(8,128)(2,1)S(1)}, u32[]{:S(2)}) copy-start(bf16[512,128]{1,0:T(8,128)(2,1)S(1)} %get-tuple-element.167) | copy-start | bytes 393220
  163.6 22.3 %collective-permute-start.11 = (bf16[512,256]{1,0:T(8,128)(2,1)S(1)}, bf16[512,256]{1,0:T(8,128)(2,1)S(1)}, u32[]{:S(2)}, u32[]{:S(2)}) collective-permute-start(bf16[512,256]{1,0:T(8,128)(2,1)S(1)} %pad_maximum_fusion.9), channel_id=1, source_target_pairs={{0,4},{4,8},{8,12},{12,16},{16,20},{20,24},{24,28},{1,5},{5,9},{9,... | collective-permute-start | bytes 786440 | tf_op jit(solution)/shard_map/ppermute | solution.py:15
  164.9 14.4 %collective-permute-start = (bf16[512]{0:T(512)(128)(2,1)S(1)}, bf16[512]{0:T(512)(128)(2,1)S(1)}, u32[]{:S(2)}, u32[]{:S(2)}) collective-permute-start(bf16[512]{0:T(512)(128)(2,1)S(1)} %add_convert_fusion.1), channel_id=1, source_target_pairs={{0,4},{4,8},{8,12},{12,16},{16,20},{20,24},{24,28},{1,5},{5,9},{9,... | collective-permute-start | bytes 3080 | tf_op jit(solution)/shard_map/ppermute | solution.py:15
  179.4 14.7 %collective-permute-start.12 = (bf16[512,256]{1,0:T(8,128)(2,1)S(1)}, bf16[512,256]{1,0:T(8,128)(2,1)S(1)}, u32[]{:S(2)}, u32[]{:S(2)}) collective-permute-start(bf16[512,256]{1,0:T(8,128)(2,1)S(1)} %slice.309), channel_id=1, source_target_pairs={{0,4},{4,8},{8,12},{12,16},{16,20},{20,24},{24,28},{1,5},{5,9},{9,... | collective-permute-start | bytes 786440 | tf_op jit(solution)/shard_map/ppermute | solution.py:15
  194.8 17.6 %copy-start.15 = (bf16[512,256]{1,0:T(8,128)(2,1)}, bf16[512,256]{1,0:T(8,128)(2,1)S(1)}, u32[]{:S(2)}) copy-start(bf16[512,256]{1,0:T(8,128)(2,1)S(1)} %convolution_convert_fusion.9) | copy-start | bytes 786436
  194.8 18.5 %copy-start.3 = (bf16[128,1152]{1,0:T(8,128)(2,1)S(1)}, bf16[128,1152]{1,0:T(8,128)(2,1)}, u32[]{:S(2)}) copy-start(bf16[128,1152]{1,0:T(8,128)(2,1)} %param.23) | copy-start | bytes 884740
  196.7 17.4 %copy-start.29 = (f32[1152]{0:T(1024)S(1)}, f32[1152]{0:T(1024)}, u32[]{:S(2)}) copy-start(f32[1152]{0:T(1024)} %get-tuple-element.125) | copy-start | bytes 13828
  196.8 6.4 collective-permute-start.15
  196.8 15.6 %collective-permute-start.14 = (bf16[128,1152]{1,0:T(8,128)(2,1)S(1)}, bf16[128,1152]{1,0:T(8,128)(2,1)S(1)}, u32[]{:S(2)}, u32[]{:S(2)}) collective-permute-start(bf16[128,1152]{1,0:T(8,128)(2,1)S(1)} %get-tuple-element.159), channel_id=1, source_target_pairs={{0,2},{1,3},{2,0},{3,1},{4,6},{5,7},{6,4},{7,5},{8,10},{9,11},{10,... | collective-permute-start | bytes 884744 | tf_op jit(solution)/shard_map/ppermute | solution.py:20
  198.4 14.1 %collective-permute-start.13 = (bf16[128,1152]{1,0:T(8,128)(2,1)S(1)}, bf16[128,1152]{1,0:T(8,128)(2,1)S(1)}, u32[]{:S(2)}, u32[]{:S(2)}) collective-permute-start(bf16[128,1152]{1,0:T(8,128)(2,1)S(1)} %get-tuple-element.157), channel_id=1, source_target_pairs={{0,1},{1,2},{2,3},{3,0},{4,5},{5,6},{6,7},{7,4},{8,9},{9,10},{10,1... | collective-permute-start | bytes 884744 | tf_op jit(solution)/shard_map/ppermute | solution.py:20
  214.2 8.7 %collective-permute-start.18 = (bf16[128,1152]{1,0:T(8,128)(2,1)S(1)}, bf16[128,1152]{1,0:T(8,128)(2,1)S(1)}, u32[]{:S(2)}, u32[]{:S(2)}) collective-permute-start(bf16[128,1152]{1,0:T(8,128)(2,1)S(1)} %multiply_convert_fusion.3), channel_id=1, source_target_pairs={{0,1},{1,2},{2,3},{3,0},{4,5},{5,6},{6,7},{7,4},{8,9},{9,10},{10,1... | collective-permute-start | bytes 884744 | tf_op jit(solution)/shard_map/ppermute | solution.py:20
  214.3 9.9 %collective-permute-start.17 = (bf16[128,1152]{1,0:T(8,128)(2,1)S(1)}, bf16[128,1152]{1,0:T(8,128)(2,1)S(1)}, u32[]{:S(2)}, u32[]{:S(2)}) collective-permute-start(bf16[128,1152]{1,0:T(8,128)(2,1)S(1)} %multiply_convert_fusion.3), channel_id=1, source_target_pairs={{0,2},{1,3},{2,0},{3,1},{4,6},{5,7},{6,4},{7,5},{8,10},{9,11},{10,... | collective-permute-start | bytes 884744 | tf_op jit(solution)/shard_map/ppermute | solution.py:20
  214.9 13.0 %collective-permute-start.16 = (bf16[128,1152]{1,0:T(8,128)(2,1)S(1)}, bf16[128,1152]{1,0:T(8,128)(2,1)}, u32[]{:S(2)}, u32[]{:S(2)}) collective-permute-start(bf16[128,1152]{1,0:T(8,128)(2,1)S(1)} %multiply_convert_fusion.3), channel_id=1, source_target_pairs={{0,3},{1,0},{2,1},{3,2},{4,7},{5,4},{6,5},{7,6},{8,11},{9,8},{10,9... | collective-permute-start | bytes 884744 | tf_op jit(solution)/shard_map/ppermute | solution.py:20
  260.1 6.4 collective-permute-start.21
  260.2 15.5 %collective-permute-start.20 = (bf16[128,1152]{1,0:T(8,128)(2,1)S(1)}, bf16[128,1152]{1,0:T(8,128)(2,1)S(1)}, u32[]{:S(2)}, u32[]{:S(2)}) collective-permute-start(bf16[128,1152]{1,0:T(8,128)(2,1)S(1)} %get-tuple-element.156), channel_id=1, source_target_pairs={{0,2},{1,3},{2,0},{3,1},{4,6},{5,7},{6,4},{7,5},{8,10},{9,11},{10,... | collective-permute-start | bytes 884744 | tf_op jit(solution)/shard_map/ppermute | solution.py:20
  261.7 29.9 %copy-start.81 = (bf16[512,1728]{0,1:T(8,128)(2,1)S(1)}, bf16[512,1728]{0,1:T(8,128)(2,1)}, u32[]{:S(2)}) copy-start(bf16[512,1728]{0,1:T(8,128)(2,1)} %get-tuple-element.184) | copy-start | bytes 5308420
  261.7 14.1 %collective-permute-start.19 = (bf16[128,1152]{1,0:T(8,128)(2,1)S(1)}, bf16[128,1152]{1,0:T(8,128)(2,1)S(1)}, u32[]{:S(2)}, u32[]{:S(2)}) collective-permute-start(bf16[128,1152]{1,0:T(8,128)(2,1)S(1)} %get-tuple-element.154), channel_id=1, source_target_pairs={{0,1},{1,2},{2,3},{3,0},{4,5},{5,6},{6,7},{7,4},{8,9},{9,10},{10,1... | collective-permute-start | bytes 884744 | tf_op jit(solution)/shard_map/ppermute | solution.py:20
  277.9 18.1 %copy-start.70 = (bf16[1728,1152]{0,1:T(8,128)(2,1)S(1)}, bf16[1728,1152]{0,1:T(8,128)(2,1)}, u32[]{:S(2)}) copy-start(bf16[1728,1152]{0,1:T(8,128)(2,1)} %all-gather.5.cloned.1.call-done) | copy-start | bytes 11943940
  277.9 18.1 %copy-start.80 = (f32[512,1728]{0,1:T(8,128)S(1)}, f32[512,1728]{0,1:T(8,128)}, u32[]{:S(2)}) copy-start(f32[512,1728]{0,1:T(8,128)} %copy-done.79) | copy-start | bytes 10616836
  277.9 8.8 %collective-permute-start.24 = (bf16[128,1152]{1,0:T(8,128)(2,1)S(1)}, bf16[128,1152]{1,0:T(8,128)(2,1)S(1)}, u32[]{:S(2)}, u32[]{:S(2)}) collective-permute-start(bf16[128,1152]{1,0:T(8,128)(2,1)S(1)} %get-tuple-element.160), channel_id=1, source_target_pairs={{0,1},{1,2},{2,3},{3,0},{4,5},{5,6},{6,7},{7,4},{8,9},{9,10},{10,1... | collective-permute-start | bytes 884744 | tf_op jit(solution)/shard_map/ppermute | solution.py:20
  277.9 9.9 %collective-permute-start.23 = (bf16[128,1152]{1,0:T(8,128)(2,1)S(1)}, bf16[128,1152]{1,0:T(8,128)(2,1)S(1)}, u32[]{:S(2)}, u32[]{:S(2)}) collective-permute-start(bf16[128,1152]{1,0:T(8,128)(2,1)S(1)} %get-tuple-element.160), channel_id=1, source_target_pairs={{0,2},{1,3},{2,0},{3,1},{4,6},{5,7},{6,4},{7,5},{8,10},{9,11},{10,... | collective-permute-start | bytes 884744 | tf_op jit(solution)/shard_map/ppermute | solution.py:20
  278.5 13.1 %collective-permute-start.22 = (bf16[128,1152]{1,0:T(8,128)(2,1)S(1)}, bf16[128,1152]{1,0:T(8,128)(2,1)S(1)}, u32[]{:S(2)}, u32[]{:S(2)}) collective-permute-start(bf16[128,1152]{1,0:T(8,128)(2,1)S(1)} %get-tuple-element.160), channel_id=1, source_target_pairs={{0,3},{1,0},{2,1},{3,2},{4,7},{5,4},{6,5},{7,6},{8,11},{9,8},{10,9... | collective-permute-start | bytes 884744 | tf_op jit(solution)/shard_map/ppermute | solution.py:20
  291.6 21.1 %slice-start.1 = ((s8[8257536]{0:T(1024)(128)(4,1)}), s8[4194304]{0:T(1024)(128)(4,1)S(1)}, s32[]{:S(2)}) async-start(s8[8257536]{0:T(1024)(128)(4,1)} %bitcast.64), calls=%async_computation.11 | async-start | bytes 8388608
  336.3 191.4 %reduce-scatter.15.cloned.1.call-start = ((), (), s32[]{:S(2)}) async-start(), calls=%async_computation.7 | async-start | bytes 4644864
  342.9 275.7 %reduce-scatter.17.cloned.1.call-start = ((), (), s32[]{:S(2)}) async-start(), calls=%async_computation.8 | async-start | bytes 4644864
  345.0 9.9 %collective-permute-start.27 = (bf16[128,1152]{1,0:T(8,128)(2,1)}, bf16[128,1152]{1,0:T(8,128)(2,1)}, u32[]{:S(2)}, u32[]{:S(2)}) collective-permute-start(bf16[128,1152]{1,0:T(8,128)(2,1)} %get-tuple-element.152), channel_id=1, source_target_pairs={{0,3},{1,0},{2,1},{3,2},{4,7},{5,4},{6,5},{7,6},{8,11},{9,8},{10,9... | collective-permute-start | bytes 884744 | tf_op jit(solution)/shard_map/ppermute | solution.py:20
  346.9 15.4 %collective-permute-start.26 = (bf16[128,1152]{1,0:T(8,128)(2,1)}, bf16[128,1152]{1,0:T(8,128)(2,1)}, u32[]{:S(2)}, u32[]{:S(2)}) collective-permute-start(bf16[128,1152]{1,0:T(8,128)(2,1)} %get-tuple-element.153), channel_id=1, source_target_pairs={{0,2},{1,3},{2,0},{3,1},{4,6},{5,7},{6,4},{7,5},{8,10},{9,11},{10,... | collective-permute-start | bytes 884744 | tf_op jit(solution)/shard_map/ppermute | solution.py:20
  348.4 14.0 %collective-permute-start.25 = (bf16[128,1152]{1,0:T(8,128)(2,1)}, bf16[128,1152]{1,0:T(8,128)(2,1)}, u32[]{:S(2)}, u32[]{:S(2)}) collective-permute-start(bf16[128,1152]{1,0:T(8,128)(2,1)} %get-tuple-element.151), channel_id=1, source_target_pairs={{0,1},{1,2},{2,3},{3,0},{4,5},{5,6},{6,7},{7,4},{8,9},{9,10},{10,1... | collective-permute-start | bytes 884744 | tf_op jit(solution)/shard_map/ppermute | solution.py:20
  354.8 340.2 %reduce-scatter.19.cloned.1.call-start = ((), (), s32[]{:S(2)}) async-start(), calls=%async_computation.9 | async-start | bytes 2985984
  366.8 7.4 %collective-permute-start.28 = (bf16[128,1152]{1,0:T(8,128)(2,1)S(1)}, bf16[128,1152]{1,0:T(8,128)(2,1)S(1)}, u32[]{:S(2)}, u32[]{:S(2)}) collective-permute-start(bf16[128,1152]{1,0:T(8,128)(2,1)S(1)} %get-tuple-element.132), channel_id=1, source_target_pairs={{0,3},{1,0},{2,1},{3,2},{4,7},{5,4},{6,5},{7,6},{8,11},{9,8},{10,9... | collective-permute-start | bytes 884744 | tf_op jit(solution)/shard_map/ppermute | solution.py:20
  366.9 13.6 %collective-permute-start.29 = (bf16[128,1152]{1,0:T(8,128)(2,1)S(1)}, bf16[128,1152]{1,0:T(8,128)(2,1)S(1)}, u32[]{:S(2)}, u32[]{:S(2)}) collective-permute-start(bf16[128,1152]{1,0:T(8,128)(2,1)S(1)} %get-tuple-element.132), channel_id=1, source_target_pairs={{0,2},{1,3},{2,0},{3,1},{4,6},{5,7},{6,4},{7,5},{8,10},{9,11},{10,... | collective-permute-start | bytes 884744 | tf_op jit(solution)/shard_map/ppermute | solution.py:20
  367.5 14.1 %collective-permute-start.30 = (bf16[128,1152]{1,0:T(8,128)(2,1)S(1)}, bf16[128,1152]{1,0:T(8,128)(2,1)S(1)}, u32[]{:S(2)}, u32[]{:S(2)}) collective-permute-start(bf16[128,1152]{1,0:T(8,128)(2,1)S(1)} %get-tuple-element.132), channel_id=1, source_target_pairs={{0,1},{1,2},{2,3},{3,0},{4,5},{5,6},{6,7},{7,4},{8,9},{9,10},{10,1... | collective-permute-start | bytes 884744 | tf_op jit(solution)/shard_map/ppermute | solution.py:20
  384.0 22.9 %collective-permute-start.32 = (bf16[512,256]{1,0:T(8,128)(2,1)S(1)}, bf16[512,256]{1,0:T(8,128)(2,1)S(1)}, u32[]{:S(2)}, u32[]{:S(2)}) collective-permute-start(bf16[512,256]{1,0:T(8,128)(2,1)S(1)} %slice.307), channel_id=1, source_target_pairs={{4,0},{8,4},{12,8},{16,12},{20,16},{24,20},{28,24},{5,1},{9,5},{13... | collective-permute-start | bytes 786440 | tf_op jit(solution)/shard_map/ppermute | solution.py:15
  387.5 17.1 %collective-permute-start.31 = (bf16[512,256]{1,0:T(8,128)(2,1)S(1)}, bf16[512,256]{1,0:T(8,128)(2,1)S(1)}, u32[]{:S(2)}, u32[]{:S(2)}) collective-permute-start(bf16[512,256]{1,0:T(8,128)(2,1)S(1)} %slice.308), channel_id=1, source_target_pairs={{4,0},{8,4},{12,8},{16,12},{20,16},{24,20},{28,24},{5,1},{9,5},{13... | collective-permute-start | bytes 786440 | tf_op jit(solution)/shard_map/ppermute | solution.py:15
  410.3 12.5 %collective-permute-start.35 = (bf16[128,1152]{1,0:T(8,128)(2,1)S(1)}, bf16[128,1152]{1,0:T(8,128)(2,1)S(1)}, u32[]{:S(2)}, u32[]{:S(2)}) collective-permute-start(bf16[128,1152]{1,0:T(8,128)(2,1)S(1)} %get-tuple-element.149), channel_id=1, source_target_pairs={{0,3},{1,0},{2,1},{3,2},{4,7},{5,4},{6,5},{7,6},{8,11},{9,8},{10,9... | collective-permute-start | bytes 884744 | tf_op jit(solution)/shard_map/ppermute | solution.py:20
  410.3 15.1 %collective-permute-start.34 = (bf16[128,1152]{1,0:T(8,128)(2,1)S(1)}, bf16[128,1152]{1,0:T(8,128)(2,1)S(1)}, u32[]{:S(2)}, u32[]{:S(2)}) collective-permute-start(bf16[128,1152]{1,0:T(8,128)(2,1)S(1)} %get-tuple-element.150), channel_id=1, source_target_pairs={{0,2},{1,3},{2,0},{3,1},{4,6},{5,7},{6,4},{7,5},{8,10},{9,11},{10,... | collective-permute-start | bytes 884744 | tf_op jit(solution)/shard_map/ppermute | solution.py:20
  411.6 14.2 %collective-permute-start.33 = (bf16[128,1152]{1,0:T(8,128)(2,1)S(1)}, bf16[128,1152]{1,0:T(8,128)(2,1)}, u32[]{:S(2)}, u32[]{:S(2)}) collective-permute-start(bf16[128,1152]{1,0:T(8,128)(2,1)S(1)} %get-tuple-element.148), channel_id=1, source_target_pairs={{0,1},{1,2},{2,3},{3,0},{4,5},{5,6},{6,7},{7,4},{8,9},{9,10},{10,1... | collective-permute-start | bytes 884744 | tf_op jit(solution)/shard_map/ppermute | solution.py:20
  696.1 7.2 collective-permute-start.38
  696.2 16.9 %collective-permute-start.37 = (bf16[144,640]{0,1:T(8,128)(2,1)S(1)}, bf16[144,640]{0,1:T(8,128)(2,1)S(1)}, u32[]{:S(2)}, u32[]{:S(2)}) collective-permute-start(bf16[144,640]{0,1:T(8,128)(2,1)S(1)} %copy.69), channel_id=1, source_target_pairs={{0,2},{1,3},{2,0},{3,1},{4,6},{5,7},{6,4},{7,5},{8,10},{9,11},{10,... | collective-permute-start | bytes 552968 | tf_op jit(solution)/shard_map/ppermute | solution.py:20
  697.7 15.5 %collective-permute-start.36 = (bf16[144,640]{0,1:T(8,128)(2,1)S(1)}, bf16[144,640]{0,1:T(8,128)(2,1)S(1)}, u32[]{:S(2)}, u32[]{:S(2)}) collective-permute-start(bf16[144,640]{0,1:T(8,128)(2,1)S(1)} %copy.69), channel_id=1, source_target_pairs={{0,1},{1,2},{2,3},{3,0},{4,5},{5,6},{6,7},{7,4},{8,9},{9,10},{10,1... | collective-permute-start | bytes 552968 | tf_op jit(solution)/shard_map/ppermute | solution.py:20
  (66 other events, 388.9 us)
Sparse Core Ops, SparseCore 0:
  10.2 164.5 all-gather.2
  177.0 77.6 all-gather.4
  336.5 100.1 reduce-scatter.12
  440.5 87.2 reduce-scatter.14
  531.2 87.2 reduce-scatter.16
  624.2 70.7 reduce-scatter.18
